TPU v7x, 256 devices: a whole 4x4x8 slice. The times are simulated.
256 devices in a mesh: side: 2 (over core), shard: 128 (over z, y, x).
Axes of the slice: x: 4, y: 4, z: 8, core: 2. Of those that a mesh axis runs over, the one named last changes fastest.
Arguments:
- node_table: bfloat16 [2, 65536, 768], P('side', 'shard'), may hold values from -6 to 6
- owner: int32 [2, 32768, 1], P('side', 'shard'), may hold values from 0 to 127; in each aligned block of 256 rows (0 to 255, 256 to 511, ..., all dimensions but the last counted through in order) at most 4 rows name the same one
- local_row: int32 [2, 32768], P('side', 'shard'), may hold values from 0 to 511
- w_in: bfloat16 [2, 768, 1024], P('side'), may hold values from -0.21875 to 0.21875
- w_mid: bfloat16 [2, 1024, 1024], P('side'), may hold values from -0.1875 to 0.1875
- w_out: bfloat16 [2, 1024, 128], P('side'), may hold values from -0.1875 to 0.1875
Outputs:
- grad_in: float32 [2, 768, 1024], P('side')
- grad_mid: float32 [2, 1024, 1024], P('side')
- grad_out: float32 [2, 1024, 128], P('side')
Inputs may be any that keep to these rules, and one draw needn't show every extreme that they name: In each tower, among the 256 pairs of one device at most 4 name the same owner, and that bound is reached.
All inputs are finite; a program needn't handle non-finite values.
Results may differ from a plain program's by a relative error of at most 0.0095.
Values may be sent and summed in bfloat16 or wider, within the bound.
No kernel may reach another device: no remote copies, remote signals or barrier semaphores. Data moves between devices by JAX's collectives and lax.ppermute only.
A program may use at most 128 MiB of HBM per device.

v0:
```python
import functools
import itertools
import math

import jax
import jax.numpy as jnp
from jax import lax
from jax.experimental import pallas as pl
from jax.experimental.pallas import tpu as pltpu
from jax.sharding import Mesh, PartitionSpec as P

NZ, NY, NX = 8, 4, 4
NYX = NY * NX
N_SHARD = NZ * NYX
CAP = 4
ROWS_DEV = 512
TOK = 256
FEAT, HID, EMB = 768, 1024, 128
SPLIT = 2
LINES = CAP * SPLIT
WIDTH = FEAT // SPLIT
TOKENS = N_SHARD * TOK
UROWS = NZ * TOK
ICOLS = NYX // 2 * TOK
QUART = 4 * TOK
EXP2_SCALE = 40.0 / math.log(2.0)
GRAD_SCALE = 40.0 * 0.5 / math.sqrt(TOKENS)
WROWS = FEAT + HID + EMB
PARTS = 3
PROWS = WROWS // PARTS
LANES = HID // 128
PIECE = PROWS * LANES // N_SHARD
BF16 = jnp.bfloat16
F32 = jnp.float32
VMEM = pl.BlockSpec(memory_space=pltpu.VMEM)
SMEM = pl.BlockSpec(memory_space=pltpu.SMEM)
ANY = pl.BlockSpec(memory_space=pl.ANY)


def call(kernel, outs, in_specs, scratch=(), mib=48, spaces=None):
    return pl.pallas_call(
        kernel,
        out_shape=[jax.ShapeDtypeStruct(s, d) for s, d in outs],
        in_specs=in_specs,
        out_specs=[pl.BlockSpec(memory_space=space) for space in spaces or [pltpu.VMEM] * len(outs)],
        scratch_shapes=list(scratch),
        compiler_params=pltpu.CompilerParams(vmem_limit_bytes=mib * 2**20),
    )


def dot(a, b, dims):
    return lax.dot_general(a, b, (dims, ((), ())), preferred_element_type=F32)


NN = ((1,), (0,))
NT = ((1,), (1,))
TN = ((0,), (0,))


def iota(shape, dim):
    return lax.broadcasted_iota(jnp.int32, shape, dim)


def begin(sources, targets, sems, first=0):
    copies = [
        pltpu.make_async_copy(source, target, sems.at[first + k])
        for k, (source, target) in enumerate(zip(sources, targets))
    ]
    for copy in copies:
        copy.start()
    return copies


def request_kernel(owner_any, wanted_any, request_ref, position_ref, owner_ref, wanted_ref, sems):
    for copy in begin([owner_any, wanted_any], [owner_ref, wanted_ref], sems):
        copy.wait()
    own_row = jnp.broadcast_to(owner_ref[...].astype(F32), (TOK, TOK))
    own_col = own_row.T
    earlier = iota((TOK, TOK), 0) < iota((TOK, TOK), 1)
    same = jnp.where((own_col == own_row) & earlier, 1.0, 0.0)
    rank = jnp.sum(same, axis=0, keepdims=True)
    owners = own_row[0:1, :]
    position_ref[...] = (owners * LINES + rank * SPLIT).astype(jnp.int32)
    wanted = wanted_ref[...].astype(F32) + 1.0
    owner_hit = iota((N_SHARD, TOK), 0).astype(F32) == owners
    lanes = iota((N_SHARD, 128), 1)
    request = jnp.zeros((N_SHARD, 128), F32)
    for k in range(CAP):
        hit = jnp.where(owner_hit & (rank == float(k)), wanted, 0.0)
        slot = jnp.sum(hit, axis=1, keepdims=True)
        request = jnp.where(lanes == k, slot, request)
    request_ref[...] = request.astype(jnp.int32) - 1


def pick_kernel(incoming_ref, table_any, picked_ref, table_ref, lines_ref, sems):
    (copy,) = begin([table_any], [table_ref], sems)
    slots = N_SHARD * CAP
    spread = jnp.where(iota((slots, N_SHARD), 0) // CAP == iota((slots, N_SHARD), 1), 1.0, 0.0)
    listed = lax.dot_general(
        spread,
        incoming_ref[...].astype(F32),
        (NN, ((), ())),
        precision=lax.Precision.HIGHEST,
        preferred_element_type=F32,
    )
    mine = iota((slots, 128), 0) % CAP == iota((slots, 128), 1)
    row = jnp.sum(jnp.where(mine, listed, 0.0), axis=1, keepdims=True)
    hit = jnp.where(row == iota((slots, ROWS_DEV), 1).astype(F32), 1.0, 0.0).astype(BF16)
    copy.wait()
    for h in range(SPLIT):
        for k in range(WIDTH // 128):
            lanes = slice(h * WIDTH + k * 128, h * WIDTH + (k + 1) * 128)
            lines_ref[k, pl.ds(h, slots, stride=SPLIT), :] = dot(hit, table_ref[:, lanes], NN)
    for k in range(WIDTH // 128):
        picked_ref[:, k * 128:(k + 1) * 128] = lines_ref[k].astype(BF16)


def finish(parts, half, place, halves, grads):
    n = len(parts)
    shapes = [(FEAT, HID), (HID, HID), (HID, EMB)]
    return pl.pallas_call(
        functools.partial(finish_kernel, parts, half),
        out_shape=[jax.ShapeDtypeStruct(shape, F32) for shape in shapes],
        in_specs=[SMEM] + [VMEM] * n + [ANY] * len(grads),
        out_specs=[ANY] * 3,
        scratch_shapes=[pltpu.VMEM((HROWS, HID), F32)] * n
        + [pltpu.VMEM((HID, EMB), F32), pltpu.SemaphoreType.DMA((2 * PARTS,))],
        input_output_aliases={1 + n + k: k for k in range(len(grads))},
        compiler_params=pltpu.CompilerParams(vmem_limit_bytes=16 * 2**20),
        cost_estimate=pl.CostEstimate(
            flops=0, transcendentals=0, bytes_accessed=n * SLOTS * PIECE * 128 * 6
        ),
    )(place, *halves, *grads)


def silu(v):
    return v * (1.0 / (1.0 + jnp.exp(-v)))


def slope(v):
    q = 1.0 / (1.0 + jnp.exp(-v))
    return q * (1.0 + v * (1.0 - q))


def forward_kernel(
    position_ref, arrived_any, w_in_any, w_mid_any, w_out_any,
    x_ref, u_ref, r_ref, e_ref, arrived_ref, w_in_ref, w_mid_ref, w_out_ref, sems,
):
    first = begin([arrived_any], [arrived_ref], sems, 3)
    loads = begin([w_in_any, w_mid_any, w_out_any], [w_in_ref, w_mid_ref, w_out_ref], sems)
    lines = iota((N_SHARD * LINES, TOK), 0)
    hits = [
        jnp.where(lines == position_ref[...] + h, 1.0, 0.0).astype(BF16) for h in range(SPLIT)
    ]
    first[0].wait()
    arrived = arrived_ref[...]
    x = jnp.concatenate([dot(hit, arrived, TN) for hit in hits], axis=1).astype(BF16)
    x_ref[...] = x
    loads[0].wait()
    z1 = dot(x, w_in_ref[...], NN)
    loads[1].wait()
    z2 = dot(silu(z1).astype(BF16), w_mid_ref[...], NN)
    loads[2].wait()
    z3 = dot(silu(z2).astype(BF16), w_out_ref[...], NN)
    r = lax.rsqrt(jnp.sum(z3 * z3, axis=1, keepdims=True) + 1e-6)
    u = z3 * r
    u_ref[...] = u
    r_ref[...] = jnp.broadcast_to(r, (TOK, EMB))
    e_ref[...] = u.astype(BF16)


CHUNK = TOK


def choose(side_ref, pieces):
    first = side_ref[0] == 0
    near, far, rest_near, rest_far, sent_near, sent_far = [piece[...] for piece in pieces]
    users = [jnp.where(first, near, sent_near), jnp.where(first, far, sent_far)]
    items = [jnp.where(first, sent_near, rest_near), jnp.where(first, sent_far, rest_far)]
    return users, jnp.concatenate(items, axis=0)


def rows_of(users, c):
    at = c * CHUNK % QUART
    return users[c * CHUNK // QUART][at:at + CHUNK, :]


LROWS = UROWS // 128


def sums_kernel(side_ref, *refs):
    keep_ref, send_ref = refs[6:]
    users, items = choose(side_ref, refs[:6])
    cols = jnp.zeros((8, ICOLS), F32)
    rows = []
    for c in range(NZ):
        expo = jnp.exp2(dot(rows_of(users, c), items, NT) * EXP2_SCALE)
        cols = cols + jnp.sum(expo.reshape(CHUNK // 8, 8, ICOLS), axis=0)
        folded = expo[:, 0:128]
        for k in range(1, ICOLS // 128):
            folded = folded + expo[:, k * 128:(k + 1) * 128]
        rows.append(jnp.sum(folded.T, axis=0, keepdims=True))
    rows = jnp.concatenate(rows, axis=1)
    cols = jnp.sum(cols, axis=0, keepdims=True)
    first = side_ref[0] == 0
    keep, send = jnp.where(first, rows, cols), jnp.where(first, cols, rows)
    for k in range(LROWS):
        keep_ref[k] = keep[:, k * 128:(k + 1) * 128]
        send_ref[k] = send[:, k * 128:(k + 1) * 128]


def grad_kernel(side_ref, *refs):
    total_ref, sent_ref, keep_ref, send_ref, away_ref, grad_ref, turned_ref = refs[6:]
    users, items = choose(side_ref, refs[:6])
    first = side_ref[0] == 0
    col = [jnp.where(first, sent_ref[k], total_ref[LROWS + k]) for k in range(LROWS)]
    col_inv = 1.0 / jnp.concatenate(col, axis=1)
    for c in range(NZ):
        chunk = rows_of(users, c)
        scores = dot(chunk, items, NT)
        places = range(c * CHUNK // 128, (c + 1) * CHUNK // 128)
        totals = [jnp.where(first, total_ref[k], sent_ref[k]) for k in places]
        inv = jnp.broadcast_to(1.0 / jnp.concatenate(totals, axis=1), (128, CHUNK)).T[:, 0:1]
        grad_ref[...] = jnp.exp2(scores * EXP2_SCALE) * (inv + col_inv)
        if c == 0:
            own = jnp.where(first, 2.0, 0.0)
            eye = jnp.where(iota((TOK, TOK), 0) == iota((TOK, TOK), 1), own, 0.0)
            grad_ref[:, 0:TOK] = grad_ref[:, 0:TOK] - eye
        grad = grad_ref[...].astype(BF16)
        keep_ref[c * CHUNK:(c + 1) * CHUNK, :] = dot(grad, items, NN) * GRAD_SCALE
        term = dot(chunk, grad, TN)
        if c == 0:
            turned_ref[...] = term
        else:
            turned_ref[...] += term
    for c in range(NZ):
        rows = slice(c * CHUNK, (c + 1) * CHUNK)
        of_items = (turned_ref[:, rows].T * GRAD_SCALE).astype(BF16)
        away_ref[rows, :] = of_items
        send_ref[rows, :] = jnp.where(first, of_items, keep_ref[rows, :].astype(BF16))


def piece_at(part, slot, code):
    piece = slot ^ code
    row = pl.multiple_of(part * PROWS + lax.shift_right_logical(piece, 3) * PIECE, 8)
    lane = pl.multiple_of(lax.bitwise_and(piece, LANES - 1) * 128, 128)
    return pl.ds(row, PIECE), pl.ds(lane, 128)


SLOTS = N_SHARD // 2


def slopes_kernel(
    x_ref, w_in_any, w_mid_any, h1_ref, h2_ref, s1_ref, s2_ref, w_in_ref, w_mid_ref, sems
):
    loads = begin([w_in_any, w_mid_any], [w_in_ref, w_mid_ref], sems)
    loads[0].wait()
    z1 = dot(x_ref[...], w_in_ref[...], NN)
    h1 = silu(z1).astype(BF16)
    h1_ref[...] = h1
    s1_ref[...] = slope(z1)
    loads[1].wait()
    z2 = dot(h1, w_mid_ref[...], NN)
    h2_ref[...] = silu(z2).astype(BF16)
    s2_ref[...] = slope(z2)


def backward_kernel(
    place_ref, keep_ref, sent0_ref, sent1_ref, sent2_ref, u_ref, r_ref,
    x_ref, h1_ref, h2_ref, s1_ref, s2_ref, w_mid_any, w_out_any, *rest,
):
    send_refs, keep_refs = rest[:PARTS], rest[PARTS:2 * PARTS]
    sums_ref, w_mid_ref, w_out_ref, sems = rest[2 * PARTS:]
    loads = begin([w_out_any, w_mid_any], [w_out_ref, w_mid_ref], sems)
    g = keep_ref[...] + sent0_ref[...].astype(F32)
    g = g + sent1_ref[...].astype(F32) + sent2_ref[...].astype(F32)
    u = u_ref[...]
    along = jnp.sum(g * u, axis=1, keepdims=True)
    dz3 = ((g - u * along) * r_ref[...]).astype(BF16)
    sums_ref[FEAT + HID:, :] = dot(dz3, h2_ref[...], TN)
    loads[0].wait()
    dz2 = (dot(dz3, w_out_ref[...], NT) * s2_ref[...]).astype(BF16)
    sums_ref[FEAT:FEAT + HID, :] = dot(h1_ref[...], dz2, TN)
    loads[1].wait()
    dz1 = (dot(dz2, w_mid_ref[...], NT) * s1_ref[...]).astype(BF16)
    sums_ref[0:FEAT, :] = dot(x_ref[...], dz1, TN)
    for part in range(PARTS):
        code = place_ref[part]
        for slot in range(SLOTS):
            keep_refs[part][slot] = sums_ref[piece_at(part, slot, code)].astype(BF16)
            send_refs[part][slot] = sums_ref[piece_at(part, SLOTS + slot, code)].astype(BF16)


HROWS = PROWS // 2
GRADS = ((0, FEAT), (FEAT, FEAT + HID), (FEAT + HID, WROWS))


def finish_kernel(parts, half, place_ref, *rest):
    n = len(parts)
    refs, rest = rest[:n], rest[n:] if half == 0 else rest[n + 3:]
    outs, rows_refs, turned_ref, sems = rest[:3], rest[3:3 + n], rest[3 + n], rest[4 + n]

    def copies_of(part, k, rows_ref, turn=True):
        base = part * PROWS + k * HROWS
        copies = []
        for out, (start, stop) in zip(outs, GRADS):
            low, high = max(start, base), min(stop, base + HROWS)
            if low >= high:
                continue
            source = rows_ref.at[low - base:high - base, :]
            target = out.at[low - start:high - start, :]
            if start == GRADS[2][0]:
                if turn:
                    turned_ref[...] = rows_ref[low - base:high - base, :].T
                source, target = turned_ref, out
            copies.append(pltpu.make_async_copy(source, target, sems.at[2 * part + len(copies)]))
        return copies

    for part, ref, rows_ref in zip(parts, refs, rows_refs):
        code = place_ref[part]
        for slot in range(SLOTS):
            piece = lax.bitwise_and(slot ^ code, SLOTS - 1)
            row = pl.multiple_of(lax.shift_right_logical(piece, 3) * PIECE, 8)
            lane = pl.multiple_of(lax.bitwise_and(piece, LANES - 1) * 128, 128)
            rows_ref[pl.ds(row, PIECE), pl.ds(lane, 128)] = ref[slot].astype(F32)
        for k in range(2):
            @pl.when((lax.shift_right_logical(code, 6) ^ half) == k)
            def _():
                for copy in copies_of(part, k, rows_ref):
                    copy.start()
    for part, rows_ref in zip(parts, rows_refs):
        for k in range(2):
            @pl.when((lax.shift_right_logical(place_ref[part], 6) ^ half) == k)
            def _():
                for copy in copies_of(part, k, rows_ref, False):
                    copy.wait()


ALL = ("z", "y", "x")
AXES = ("side",) + ALL
SIZES = {"side": 2, "z": NZ, "y": NY, "x": NX}
PLACES = list(itertools.product(*(range(SIZES[axis]) for axis in AXES)))
NUMBERS = {place: k for k, place in enumerate(PLACES)}


def exchange(value, axes):
    return lax.all_to_all(value, axes, split_axis=0, concat_axis=0, tiled=True)


def swap(value):
    return lax.ppermute(value, "side", [(0, 1), (1, 0)])


def gray(i):
    return i ^ (i >> 1)


def across(value, *flips):
    pairs = []
    for place, number in NUMBERS.items():
        if flips[place[0]] is None:
            continue
        other = []
        for axis, i in zip(AXES, place):
            at = {gray(k): k for k in range(SIZES[axis])}
            other.append(at[gray(i) ^ flips[place[0]].get(axis, 0)])
        pairs.append((number, NUMBERS[tuple(other)]))
    return lax.ppermute(value, AXES, pairs)


def both(value, **flips):
    return across(value, flips, flips)


def code_of(i, side, n):
    return gray((i + side) % n)


def trade(value, **flips):
    pairs = []
    for place, number in NUMBERS.items():
        other = [place[0]]
        for axis, i in zip(ALL, place[1:]):
            n = SIZES[axis]
            at = {code_of(k, place[0], n): k for k in range(n)}
            other.append(at[code_of(i, place[0], n) ^ flips.get(axis, 0)])
        pairs.append((number, NUMBERS[tuple(other)]))
    return lax.ppermute(value, AXES, pairs)


PLANE_FOURS = (dict(y=2), dict(x=2), dict(x=2, y=2))
HEADS = (dict(x=1), dict(y=1), dict(z=1))
TAIL = (("x", 1), ("y", 1), ("z", 2), ("z", 1))


def heads_of(part):
    return HEADS[part:] + HEADS[:part]


def mark_of(part):
    bits = [(axis, 0) for head in heads_of(part) for axis in head] + list(TAIL)
    code = 0
    for axis, bit in bits:
        own = code_of(lax.axis_index(axis), lax.axis_index("side"), SIZES[axis])
        code = code * 2 + ((own >> bit) & 1)
    return code


def turned(value, axis, d):
    return jnp.concatenate(
        [lax.slice_in_dim(value, k ^ d, (k ^ d) + 1, axis=axis) for k in range(4)], axis=axis
    )


def halves(value):
    n = value.shape[0] // 2
    return value[:n], value[n:].astype(BF16)


def sum_weights(sends, keeps):
    sums = []
    for part in range(PARTS):
        keep, send = keeps[part], sends[part]
        for step in range(len(HEADS)):
            value = keep.astype(F32) + trade(send, **heads_of(part)[step]).astype(F32)
            if step < len(HEADS) - 1:
                keep, send = halves(value)
        sums.append(value)
    value = jnp.stack(sums).reshape(PARTS, 4, 4, PIECE, 128)
    sent = value.astype(BF16)
    got = [trade(sent[:, d + 1], **flips) for d, flips in enumerate(PLANE_FOURS)]
    value = value[:, 0] + got[0].astype(F32) + got[1].astype(F32) + got[2].astype(F32)
    for bit, axis in ((4, 1), (2, 2)):
        mine = value.astype(BF16)
        got = trade(mine, z=bit).reshape(PARTS, 2, 2, PIECE, 128)
        mine = mine.astype(F32).reshape(PARTS, 2, 2, PIECE, 128)
        value = (mine + jnp.flip(got, axis).astype(F32)).reshape(PARTS, 4, PIECE, 128)
    return value.astype(BF16)


def spread_weights(value):
    value = jnp.concatenate([value] + [trade(value, **flips) for flips in PLANE_FOURS], axis=1)
    pairs = []
    for part in range(PARTS):
        mine = value[part]
        heads = heads_of(part)[::-1]
        for head in heads[:-1]:
            mine = jnp.concatenate([mine, trade(mine, **head)], axis=0)
        pairs += [mine, trade(mine, **heads[-1])]
    return pairs


FOURS = [({"z": 2 * d}, {"x": d}) for d in (1, 2, 3)]


def sum_all(keep, send, side):
    sent = swap(send)
    value = jnp.concatenate([sent + jnp.where(side == 0, keep, 0.0), keep])
    value = value.reshape(4, 4, TOK // 128, 1, 128)
    got = [turned(across(value, *flips), 1, d + 1) for d, flips in enumerate(FOURS)]
    value = (value + got[0]) + (got[1] + got[2])
    got = [turned(across(value, {"z": 1} if d == 1 else None, {"y": d}), 0, d) for d in (1, 2, 3)]
    value = ((value + got[0]) + (got[1] + got[2])).reshape(2 * LROWS, 1, 128)
    return value, swap(value[:LROWS])


def on_device(node_table, owner, local_row, w_in, w_mid, w_out):
    side = lax.axis_index("side").astype(jnp.int32)[None]
    place = jnp.stack([mark_of(part) for part in range(PARTS)]).astype(jnp.int32)
    table, weight_in, weight_mid, weight_out = node_table[0], w_in[0], w_mid[0], w_out[0]

    request, position = call(
        request_kernel,
        [((N_SHARD, 128), jnp.int32), ((1, TOK), jnp.int32)],
        [ANY, ANY],
        [pltpu.VMEM((1, TOK), jnp.int32)] * 2 + [pltpu.SemaphoreType.DMA((2,))],
        mib=63,
    )(owner.reshape(1, TOK), local_row)
    incoming = exchange(request.reshape(N_SHARD, 1, 128), ALL).reshape(N_SHARD, 128)
    (picked,) = call(
        pick_kernel,
        [((N_SHARD * LINES, WIDTH), BF16)],
        [VMEM, ANY],
        [
            pltpu.VMEM((ROWS_DEV, FEAT), BF16),
            pltpu.VMEM((WIDTH // 128, N_SHARD * LINES, 128), F32),
            pltpu.SemaphoreType.DMA((1,)),
        ],
    )(incoming, table)
    arrived = exchange(picked.reshape(N_SHARD, LINES, WIDTH), ALL).reshape(N_SHARD * LINES, WIDTH)
    weights = [pltpu.VMEM((FEAT, HID), BF16), pltpu.VMEM((HID, HID), BF16), pltpu.VMEM((HID, EMB), BF16)]
    x, u, r, e = call(
        forward_kernel,
        [
            ((TOK, FEAT), BF16), ((TOK, EMB), F32), ((TOK, EMB), F32), ((TOK, EMB), BF16),
        ],
        [VMEM, ANY, ANY, ANY, ANY],
        [pltpu.VMEM((N_SHARD * LINES, WIDTH), BF16)] + weights + [pltpu.SemaphoreType.DMA((4,))],
        mib=63,
    )(position, arrived, weight_in, weight_mid, weight_out)

    near = jnp.concatenate([e] + [across(e, *flips) for flips in FOURS])
    far = across(near, {"z": 1}, {"y": 1})
    rest = [across(near, None, {"y": d}) for d in (2, 3)]
    held, near_sent = lax.optimization_barrier((far, near))
    pieces = [near, far] + rest + [swap(near_sent), swap(held)]
    sums = call(
        sums_kernel, [((LROWS, 1, 128), F32)] * 2, [SMEM] + [VMEM] * 6, mib=32
    )(side, *pieces)
    sums = sum_all(*sums, side[0])

    keep, send, away = call(
        grad_kernel,
        [((UROWS, EMB), F32), ((UROWS, EMB), BF16), ((ICOLS, EMB), BF16)],
        [SMEM] + [VMEM] * 8,
        [pltpu.VMEM((CHUNK, ICOLS), F32), pltpu.VMEM((EMB, ICOLS), F32)],
        mib=32,
    )(side, *pieces, *sums)
    got = [across(away[(d - 2) * QUART:(d - 1) * QUART], None, {"y": d}) for d in (2, 3)]
    grad = jnp.where(side[0] == 0, keep, 0.0) + swap(send).astype(F32)
    got.append(across(grad[QUART:].astype(BF16), {"z": 1}, {"y": 1}))
    grad = grad[:QUART] + got[2].astype(F32) + got[0].astype(F32) + got[1].astype(F32)
    grad = grad.reshape(4, TOK, EMB)
    got = [across(grad[d + 1].astype(BF16), *flips) for d, flips in enumerate(FOURS)]

    wide = (TOK, HID)
    slopes = call(
        slopes_kernel,
        [(wide, BF16), (wide, BF16), (wide, F32), (wide, F32)],
        [VMEM, ANY, ANY],
        weights[:2] + [pltpu.SemaphoreType.DMA((2,))],
        mib=16,
    )(x, weight_in, weight_mid)
    slots = (SLOTS, PIECE, 128)
    sums = call(
        backward_kernel,
        [(slots, BF16)] * (2 * PARTS),
        [SMEM] + [VMEM] * 11 + [ANY] * 2,
        [pltpu.VMEM((WROWS, HID), F32)] + weights[1:] + [pltpu.SemaphoreType.DMA((2,))],
        mib=32,
    )(place, grad[0], *got, u, r, x, *slopes, weight_mid, weight_out)
    pairs = spread_weights(sum_weights(sums[:PARTS], sums[PARTS:]))
    grads = finish(tuple(range(PARTS)), 0, place, pairs[0::2], ())
    grads = finish(tuple(range(PARTS)), 1, place, pairs[1::2], grads)
    return tuple(g[None] for g in grads)


def solution(mesh):
    cube = Mesh(mesh.devices.reshape(2, NZ, NY, NX), ("side", "z", "y", "x"))
    rows = P("side", ALL, None)
    whole = P("side", None, None)
    return jax.shard_map(
        on_device,
        mesh=cube,
        in_specs=(rows, rows, P("side", ALL), whole, whole, whole),
        out_specs=(whole, whole, whole),
        check_vma=False,
    )
```

profile of v0, /device:TPU:2, one launch (start us, length us, event | category | flops | bytes accessed | tf_op | source)
XLA Modules:
  0.0 246.0 jit_solution(6577729027548858124)
XLA Ops:
  0.6 1.6 shard_map.85
  2.3 26.7 %all_to_all.10 = s32[128,1,128]{2,1,0:T(1,128)S(1)} all-to-all(s32[128,1,128]{2,1,0:T(1,128)} %bitcast.95), channel_id=1, replica_groups=mesh['side'=2,'z'=8,'y'=4,'x'=4] {'z','y','x'}, dimensions={0} | all-to-all | bytes 131072 | tf_op jit(solution)/shard_map/all_to_all | solution.py:347
  30.1 2.0 shard_map.86
  32.1 30.9 %all_to_all.11 = bf16[128,8,384]{2,1,0:T(8,128)(2,1)} all-to-all(bf16[128,8,384]{2,1,0:T(8,128)(2,1)S(1)} %bitcast.66), channel_id=1, replica_groups=mesh['side'=2,'z'=8,'y'=4,'x'=4] {'z','y','x'}, dimensions={0} | all-to-all | bytes 1572864 | tf_op jit(solution)/shard_map/all_to_all | solution.py:347
  63.0 5.1 %shard_map.87 = (bf16[256,768]{1,0:T(8,128)(2,1)}, f32[256,128]{1,0:T(8,128)}, f32[256,128]{1,0:T(8,128)}, bf16[256,128]{1,0:T(8,128)(2,1)}) custom-call(s32[1,256]{1,0:T(1,128)} %get-tuple-element.32.position_ref, bf16[1024,384]{1,0:T(8,128)(2,1)} %bitcast.73, bf16[768,1024]{1,0:T(8,128)(2,1)} %bitcast.64, bf16[1024,1024]{1,0:T(8,128)(2,1)} %bitcast.61, ...), custom_call_target="tpu_custom_call" | custom-call | tf_op jit(solution)/shard_map/pallas_call | solution.py:492
  68.2 3.4 %collective-permute-start.1 = (bf16[256,128]{1,0:T(8,128)(2,1)}, bf16[256,128]{1,0:T(8,128)(2,1)S(1)}, u32[]{:S(2)}, u32[]{:S(2)}) collective-permute-start(bf16[256,128]{1,0:T(8,128)(2,1)} %get-tuple-element.34), channel_id=1, source_target_pairs={{0,112},{1,113},{2,114},{3,115},{4,116},{5,117},{6,118},{7,119},{8... | collective-permute-start | bytes 196616 | tf_op jit(solution)/shard_map/ppermute | solution.py:368
  71.6 3.1 %collective-permute-start = (bf16[256,128]{1,0:T(8,128)(2,1)}, bf16[256,128]{1,0:T(8,128)(2,1)S(1)}, u32[]{:S(2)}, u32[]{:S(2)}) collective-permute-start(bf16[256,128]{1,0:T(8,128)(2,1)} %get-tuple-element.34), channel_id=1, source_target_pairs={{0,48},{1,49},{2,50},{3,51},{4,52},{5,53},{6,54},{7,55},{8,56},{9,... | collective-permute-start | bytes 196616 | tf_op jit(solution)/shard_map/ppermute | solution.py:368
  75.6 3.4 %collective-permute-done = bf16[256,128]{1,0:T(8,128)(2,1)S(1)} collective-permute-done((bf16[256,128]{1,0:T(8,128)(2,1)}, bf16[256,128]{1,0:T(8,128)(2,1)S(1)}, u32[]{:S(2)}, u32[]{:S(2)}) %collective-permute-start) | collective-permute-done | bytes 65568 | tf_op jit(solution)/shard_map/ppermute | solution.py:368
  80.5 5.0 %collective-permute-done.3.refs_1_ = bf16[1024,128]{1,0:T(8,128)(2,1)S(1)} collective-permute-done((bf16[1024,128]{1,0:T(8,128)(2,1)S(1)}, bf16[1024,128]{1,0:T(8,128)(2,1)S(1)}, u32[]{:S(2)}, u32[]{:S(2)}) %collective-permute-start.3) | collective-permute-done | bytes 262176 | tf_op jit(solution)/shard_map/ppermute | solution.py:368
  85.5 11.2 %collective-permute-start.7 = (bf16[1024,128]{1,0:T(8,128)(2,1)S(1)}, bf16[1024,128]{1,0:T(8,128)(2,1)S(1)}, u32[]{:S(2)}, u32[]{:S(2)}) collective-permute-start(bf16[1024,128]{1,0:T(8,128)(2,1)S(1)} %collective-permute-done.3.refs_1_), channel_id=1, source_target_pairs={{0,128},{128,0},{1,129},{129,1},{2,130},{130,2},{3,131},{131,3},{4... | collective-permute-start | bytes 786440 | tf_op jit(solution)/shard_map/ppermute | solution.py:351
  97.9 2.6 %shard_map.88 = (f32[16,1,128]{2,1,0:T(1,128)S(1)}, f32[16,1,128]{2,1,0:T(1,128)S(1)}) custom-call(s32[1]{0:T(128)} %bitcast.3.side_ref, bf16[1024,128]{1,0:T(8,128)(2,1)S(1)} %constant_dynamic-update-slice_fusion.refs_0_, bf16[1024,128]{1,0:T(8,128)(2,1)S(1)} %collective-permute-done.3.refs_1_, bf16[1024,128]{1,0:T(8,128)(2,1)S(1)} %collective-permute-done.4.refs_2_, ...), custom_call_target="tpu_custom_call" | custom-call | tf_op jit(solution)/shard_map/pallas_call | solution.py:507
  101.9 4.8 %collective-permute-start.11 = (f32[4,4,2,1,128]{4,2,1,0,3:T(2,128)S(1)}, f32[4,4,2,1,128]{4,2,1,0,3:T(2,128)S(1)}, u32[]{:S(2)}, u32[]{:S(2)}) collective-permute-start(f32[4,4,2,1,128]{4,2,1,0,3:T(2,128)S(1)} %bitcast.92), channel_id=1, source_target_pairs={{0,64},{1,65},{2,66},{3,67},{4,68},{5,69},{6,70},{7,71},{8,72},{9,... | collective-permute-start | bytes 49160 | tf_op jit(solution)/shard_map/ppermute | solution.py:368
  106.7 1.7 collective-permute-start.9
  109.7 2.6 %collective-permute-done.9 = f32[4,4,2,1,128]{4,2,1,0,3:T(2,128)S(1)} collective-permute-done((f32[4,4,2,1,128]{4,2,1,0,3:T(2,128)S(1)}, f32[4,4,2,1,128]{4,2,1,0,3:T(2,128)S(1)}, u32[]{:S(2)}, u32[]{:S(2)}) %collective-permute-start.9) | collective-permute-done | bytes 16416 | tf_op jit(solution)/shard_map/ppermute | solution.py:368
  113.8 3.7 %collective-permute-done.12 = f32[4,4,2,1,128]{4,2,1,0,3:T(2,128)S(1)} collective-permute-done((f32[4,4,2,1,128]{4,2,1,0,3:T(2,128)S(1)}, f32[4,4,2,1,128]{4,2,1,0,3:T(2,128)S(1)}, u32[]{:S(2)}, u32[]{:S(2)}) %collective-permute-start.12) | collective-permute-done | bytes 16416 | tf_op jit(solution)/shard_map/ppermute | solution.py:368
  118.8 6.1 %shard_map.89 = (f32[2048,128]{1,0:T(8,128)S(1)}, bf16[2048,128]{1,0:T(8,128)(2,1)S(1)}, bf16[2048,128]{1,0:T(8,128)(2,1)S(1)}) custom-call(s32[1]{0:T(128)} %bitcast.3.side_ref, bf16[1024,128]{1,0:T(8,128)(2,1)S(1)} %constant_dynamic-update-slice_fusion.refs_0_, bf16[1024,128]{1,0:T(8,128)(2,1)S(1)} %collective-permute-done.3.refs_1_, ...), custom_call_target="tpu_custom_call" | custom-call | tf_op jit(solution)/shard_map/pallas_call | solution.py:512
  129.6 6.7 %collective-permute-done.17 = bf16[1024,128]{1,0:T(8,128)(2,1)} collective-permute-done((bf16[1024,128]{1,0:T(8,128)(2,1)}, bf16[1024,128]{1,0:T(8,128)(2,1)}, u32[]{:S(2)}, u32[]{:S(2)}) %collective-permute-start.17) | collective-permute-done | bytes 262176 | tf_op jit(solution)/shard_map/ppermute | solution.py:368
  137.6 2.2 collective-permute-start.22
  139.8 2.2 collective-permute-start.21
  142.0 2.5 %collective-permute-start.20 = (bf16[256,128]{1,0:T(8,128)(2,1)S(1)}, bf16[256,128]{1,0:T(8,128)(2,1)S(1)}, u32[]{:S(2)}, u32[]{:S(2)}) collective-permute-start(bf16[256,128]{1,0:T(8,128)(2,1)S(1)} %get-tuple-element.75), channel_id=1, source_target_pairs={{0,48},{1,49},{2,50},{3,51},{4,52},{5,53},{6,54},{7,55},{8,56},{9,... | collective-permute-start | bytes 196616 | tf_op jit(solution)/shard_map/ppermute | solution.py:368
  144.6 1.4 copy-done.1
  146.0 2.1 shard_map.90
  148.6 4.2 %shard_map.91 = (bf16[64,40,128]{2,1,0:T(8,128)(2,1)S(1)}, bf16[64,40,128]{2,1,0:T(8,128)(2,1)S(1)}, bf16[64,40,128]{2,1,0:T(8,128)(2,1)S(1)}, bf16[64,40,128]{2...) custom-call(s32[3]{0:T(128)S(1)} %pad_add_fusion.place_ref, ...), custom_call_target="tpu_custom_call" | custom-call | tf_op jit(solution)/shard_map/pallas_call | solution.py:535
  152.8 1.5 collective-permute-start.23
  155.4 8.1 %collective-permute-done.23 = bf16[64,40,128]{2,1,0:T(8,128)(2,1)S(1)} collective-permute-done((bf16[64,40,128]{2,1,0:T(8,128)(2,1)S(1)}, bf16[64,40,128]{2,1,0:T(8,128)(2,1)S(1)}, u32[]{:S(2)}, u32[]{:S(2)}) %collective-permute-start.23) | collective-permute-done | bytes 655392 | tf_op jit(solution)/shard_map/ppermute | solution.py:388
  166.8 4.0 %collective-permute-done.24 = bf16[32,40,128]{2,1,0:T(8,128)(2,1)S(1)} collective-permute-done((bf16[32,40,128]{2,1,0:T(8,128)(2,1)S(1)}, bf16[32,40,128]{2,1,0:T(8,128)(2,1)S(1)}, u32[]{:S(2)}, u32[]{:S(2)}) %collective-permute-start.24) | collective-permute-done | bytes 327712 | tf_op jit(solution)/shard_map/ppermute | solution.py:388
  173.4 1.5 collective-permute-start.31
  174.9 1.4 collective-permute-done.25
  178.9 1.7 collective-permute-start.32
  180.6 2.2 collective-permute-start.34
  185.1 2.5 %collective-permute-done.34 = bf16[3,4,40,128]{3,2,1,0:T(8,128)(2,1)S(1)} collective-permute-done((bf16[3,4,40,128]{3,2,1,0:T(8,128)(2,1)S(1)}, bf16[3,4,40,128]{3,2,1,0:T(8,128)(2,1)S(1)}, u32[]{:S(2)}, u32[]{:S(2)}) %collective-permute-start.34) | collective-permute-done | bytes 122912 | tf_op jit(solution)/shard_map/ppermute | solution.py:388
  187.9 2.0 collective-permute-start.35
  189.9 4.4 %collective-permute-done.35 = bf16[3,4,40,128]{3,2,1,0:T(8,128)(2,1)S(1)} collective-permute-done((bf16[3,4,40,128]{3,2,1,0:T(8,128)(2,1)S(1)}, bf16[3,4,40,128]{3,2,1,0:T(8,128)(2,1)S(1)}, u32[]{:S(2)}, u32[]{:S(2)}) %collective-permute-start.35) | collective-permute-done | bytes 122912 | tf_op jit(solution)/shard_map/ppermute | solution.py:388
  194.3 2.6 %collective-permute-start.36 = (bf16[3,4,40,128]{3,2,1,0:T(8,128)(2,1)S(1)}, bf16[3,4,40,128]{3,2,1,0:T(8,128)(2,1)S(1)}, u32[]{:S(2)}, u32[]{:S(2)}) collective-permute-start(bf16[3,4,40,128]{3,2,1,0:T(8,128)(2,1)S(1)} %bitcast.86), channel_id=1, source_target_pairs={{0,48},{1,49},{2,50},{3,51},{4,52},{5,53},{6,54},{7,55},{8,56},{9,... | collective-permute-start | bytes 368648 | tf_op jit(solution)/shard_map/ppermute | solution.py:388
  196.9 4.5 %collective-permute-done.36 = bf16[3,4,40,128]{3,2,1,0:T(8,128)(2,1)S(1)} collective-permute-done((bf16[3,4,40,128]{3,2,1,0:T(8,128)(2,1)S(1)}, bf16[3,4,40,128]{3,2,1,0:T(8,128)(2,1)S(1)}, u32[]{:S(2)}, u32[]{:S(2)}) %collective-permute-start.36) | collective-permute-done | bytes 122912 | tf_op jit(solution)/shard_map/ppermute | solution.py:388
  201.4 3.9 %collective-permute-start.39 = (bf16[3,4,40,128]{3,2,1,0:T(8,128)(2,1)S(1)}, bf16[3,4,40,128]{3,2,1,0:T(8,128)(2,1)S(1)}, u32[]{:S(2)}, u32[]{:S(2)}) collective-permute-start(bf16[3,4,40,128]{3,2,1,0:T(8,128)(2,1)S(1)} %bitcast.81), channel_id=1, source_target_pairs={{0,15},{1,14},{2,13},{3,12},{4,11},{5,10},{6,9},{7,8},{8,7},{9,6},... | collective-permute-start | bytes 368648 | tf_op jit(solution)/shard_map/ppermute | solution.py:388
  206.2 2.3 collective-permute-done.39
  208.5 2.4 collective-permute-done.38
  210.9 1.4 collective-permute-done.37
  212.5 3.0 %collective-permute-start.40 = (bf16[16,40,128]{2,1,0:T(8,128)(2,1)S(1)}, bf16[16,40,128]{2,1,0:T(8,128)(2,1)S(1)}, u32[]{:S(2)}, u32[]{:S(2)}) collective-permute-start(bf16[16,40,128]{2,1,0:T(8,128)(2,1)S(1)} %get-tuple-element.69), channel_id=1, source_target_pairs={{0,16},{1,17},{2,18},{3,19},{4,20},{5,21},{6,22},{7,23},{8,24},{9,... | collective-permute-start | bytes 491528 | tf_op jit(solution)/shard_map/ppermute | solution.py:388
  215.5 4.0 %collective-permute-start.43 = (bf16[16,40,128]{2,1,0:T(8,128)(2,1)S(1)}, bf16[16,40,128]{2,1,0:T(8,128)(2,1)S(1)}, u32[]{:S(2)}, u32[]{:S(2)}) collective-permute-start(bf16[16,40,128]{2,1,0:T(8,128)(2,1)S(1)} %get-tuple-element.68), channel_id=1, source_target_pairs={{0,1},{1,0},{2,3},{3,2},{4,5},{5,4},{6,7},{7,6},{8,9},{9,8},{10,11... | collective-permute-start | bytes 491528 | tf_op jit(solution)/shard_map/ppermute | solution.py:388
  219.5 2.1 collective-permute-start.41
  225.6 2.6 %collective-permute-done.41 = bf16[32,40,128]{2,1,0:T(8,128)(2,1)S(1)} collective-permute-done((bf16[32,40,128]{2,1,0:T(8,128)(2,1)S(1)}, bf16[32,40,128]{2,1,0:T(8,128)(2,1)S(1)}, u32[]{:S(2)}, u32[]{:S(2)}) %collective-permute-start.41) | collective-permute-done | bytes 327712 | tf_op jit(solution)/shard_map/ppermute | solution.py:388
  228.4 2.4 collective-permute-start.42
  232.8 3.1 %shard_map.92 = (f32[768,1024]{1,0:T(8,128)}, f32[1024,1024]{1,0:T(8,128)}, f32[1024,128]{1,0:T(8,128)}) custom-call(s32[3]{0:T(128)S(1)} %pad_add_fusion.place_ref, bf16[64,40,128]{2,1,0:T(8,128)(2,1)S(1)} %pad_maximum_fusion.1.rest_0_, bf16[64,40,128]{2,1,0:T(8,128)(2,1)S(1)} %pad_maximum_fusion.2.rest_1_, bf16[64,40,128]{2,1,0:T(8,128)(2,1)S(1)} %pad_maximum_fusion.3.rest_2_), custom_call_target="tpu_custom_call" | custom-call | bytes 5898240 | tf_op jit(solution)/shard_map/pallas_call | solution.py:121
  235.9 3.4 %collective-permute-done.42.rest_0_ = bf16[64,40,128]{2,1,0:T(8,128)(2,1)S(1)} collective-permute-done((bf16[64,40,128]{2,1,0:T(8,128)(2,1)S(1)}, bf16[64,40,128]{2,1,0:T(8,128)(2,1)S(1)}, u32[]{:S(2)}, u32[]{:S(2)}) %collective-permute-start.42) | collective-permute-done | bytes 655392 | tf_op jit(solution)/shard_map/ppermute | solution.py:388
  239.3 2.2 collective-permute-done.45.rest_1_
  242.7 3.1 %shard_map.93 = (f32[768,1024]{1,0:T(8,128)}, f32[1024,1024]{1,0:T(8,128)}, f32[1024,128]{1,0:T(8,128)}) custom-call(s32[3]{0:T(128)S(1)} %pad_add_fusion.place_ref, bf16[64,40,128]{2,1,0:T(8,128)(2,1)S(1)} %collective-permute-done.42.rest_0_, ...), custom_call_target="tpu_custom_call", output_to_operand_aliasing={{0}: (4, {}), {1}: (5, {}), {2}: (6, {})} | custom-call | bytes 5898240 | tf_op jit(solution)/shard_map/pallas_call | solution.py:121
  (127 shorter events, 37.4 us)
Async XLA Ops:
  68.1 10.9 %collective-permute-start.2 = (bf16[256,128]{1,0:T(8,128)(2,1)}, bf16[256,128]{1,0:T(8,128)(2,1)S(1)}, u32[]{:S(2)}, u32[]{:S(2)}) collective-permute-start(bf16[256,128]{1,0:T(8,128)(2,1)} %get-tuple-element.34), channel_id=1, source_target_pairs={{0,64},{1,65},{2,66},{3,67},{4,68},{5,69},{6,70},{7,71},{8,72},{9,... | collective-permute-start | bytes 196616 | tf_op jit(solution)/shard_map/ppermute | solution.py:368
  68.2 10.7 %collective-permute-start.1 = (bf16[256,128]{1,0:T(8,128)(2,1)}, bf16[256,128]{1,0:T(8,128)(2,1)S(1)}, u32[]{:S(2)}, u32[]{:S(2)}) collective-permute-start(bf16[256,128]{1,0:T(8,128)(2,1)} %get-tuple-element.34), channel_id=1, source_target_pairs={{0,112},{1,113},{2,114},{3,115},{4,116},{5,117},{6,118},{7,119},{8... | collective-permute-start | bytes 196616 | tf_op jit(solution)/shard_map/ppermute | solution.py:368
  71.6 7.4 %collective-permute-start = (bf16[256,128]{1,0:T(8,128)(2,1)}, bf16[256,128]{1,0:T(8,128)(2,1)S(1)}, u32[]{:S(2)}, u32[]{:S(2)}) collective-permute-start(bf16[256,128]{1,0:T(8,128)(2,1)} %get-tuple-element.34), channel_id=1, source_target_pairs={{0,48},{1,49},{2,50},{3,51},{4,52},{5,53},{6,54},{7,55},{8,56},{9,... | collective-permute-start | bytes 196616 | tf_op jit(solution)/shard_map/ppermute | solution.py:368
  79.0 6.5 %collective-permute-start.3 = (bf16[1024,128]{1,0:T(8,128)(2,1)S(1)}, bf16[1024,128]{1,0:T(8,128)(2,1)S(1)}, u32[]{:S(2)}, u32[]{:S(2)}) collective-permute-start(bf16[1024,128]{1,0:T(8,128)(2,1)S(1)} %constant_dynamic-update-slice_fusion.refs_0_), channel_id=1, source_target_pairs={{0,16},{1,17},{2,18},{3,19},{4,20},{5,21},{6,22},{7,23},{8,24},{9,... | collective-permute-start | bytes 786440 | tf_op jit(solution)/shard_map/ppermute | solution.py:368
  79.1 17.6 %collective-permute-start.5 = (bf16[1024,128]{1,0:T(8,128)(2,1)S(1)}, bf16[1024,128]{1,0:T(8,128)(2,1)S(1)}, u32[]{:S(2)}, u32[]{:S(2)}) collective-permute-start(bf16[1024,128]{1,0:T(8,128)(2,1)S(1)} %constant_dynamic-update-slice_fusion.refs_0_), channel_id=1, source_target_pairs={{128,136},{129,137},{130,138},{131,139},{132,140},{133,141},{134,1... | collective-permute-start | bytes 786440 | tf_op jit(solution)/shard_map/ppermute | solution.py:368
  79.8 16.9 %collective-permute-start.4 = (bf16[1024,128]{1,0:T(8,128)(2,1)S(1)}, bf16[1024,128]{1,0:T(8,128)(2,1)S(1)}, u32[]{:S(2)}, u32[]{:S(2)}) collective-permute-start(bf16[1024,128]{1,0:T(8,128)(2,1)S(1)} %constant_dynamic-update-slice_fusion.refs_0_), channel_id=1, source_target_pairs={{128,140},{129,141},{130,142},{131,143},{132,136},{133,137},{134,1... | collective-permute-start | bytes 786440 | tf_op jit(solution)/shard_map/ppermute | solution.py:368
  85.5 11.3 %collective-permute-start.6 = (bf16[1024,128]{1,0:T(8,128)(2,1)S(1)}, bf16[1024,128]{1,0:T(8,128)(2,1)S(1)}, u32[]{:S(2)}, u32[]{:S(2)}) collective-permute-start(bf16[1024,128]{1,0:T(8,128)(2,1)S(1)} %constant_dynamic-update-slice_fusion.refs_0_), channel_id=1, source_target_pairs={{0,128},{128,0},{1,129},{129,1},{2,130},{130,2},{3,131},{131,3},{4... | collective-permute-start | bytes 786440 | tf_op jit(solution)/shard_map/ppermute | solution.py:351
  85.5 12.4 %collective-permute-start.7 = (bf16[1024,128]{1,0:T(8,128)(2,1)S(1)}, bf16[1024,128]{1,0:T(8,128)(2,1)S(1)}, u32[]{:S(2)}, u32[]{:S(2)}) collective-permute-start(bf16[1024,128]{1,0:T(8,128)(2,1)S(1)} %collective-permute-done.3.refs_1_), channel_id=1, source_target_pairs={{0,128},{128,0},{1,129},{129,1},{2,130},{130,2},{3,131},{131,3},{4... | collective-permute-start | bytes 786440 | tf_op jit(solution)/shard_map/ppermute | solution.py:351
  100.5 1.3 collective-permute-start.8
  101.8 6.6 %collective-permute-start.10 = (f32[4,4,2,1,128]{4,2,1,0,3:T(2,128)S(1)}, f32[4,4,2,1,128]{4,2,1,0,3:T(2,128)S(1)}, u32[]{:S(2)}, u32[]{:S(2)}) collective-permute-start(f32[4,4,2,1,128]{4,2,1,0,3:T(2,128)S(1)} %bitcast.91), channel_id=1, source_target_pairs={{0,112},{1,113},{2,114},{3,115},{4,116},{5,117},{6,118},{7,119},{8... | collective-permute-start | bytes 49160 | tf_op jit(solution)/shard_map/ppermute | solution.py:368
  101.9 7.7 %collective-permute-start.11 = (f32[4,4,2,1,128]{4,2,1,0,3:T(2,128)S(1)}, f32[4,4,2,1,128]{4,2,1,0,3:T(2,128)S(1)}, u32[]{:S(2)}, u32[]{:S(2)}) collective-permute-start(f32[4,4,2,1,128]{4,2,1,0,3:T(2,128)S(1)} %bitcast.92), channel_id=1, source_target_pairs={{0,64},{1,65},{2,66},{3,67},{4,68},{5,69},{6,70},{7,71},{8,72},{9,... | collective-permute-start | bytes 49160 | tf_op jit(solution)/shard_map/ppermute | solution.py:368
  106.7 5.5 %collective-permute-start.9 = (f32[4,4,2,1,128]{4,2,1,0,3:T(2,128)S(1)}, f32[4,4,2,1,128]{4,2,1,0,3:T(2,128)S(1)}, u32[]{:S(2)}, u32[]{:S(2)}) collective-permute-start(f32[4,4,2,1,128]{4,2,1,0,3:T(2,128)S(1)} %bitcast.93), channel_id=1, source_target_pairs={{0,48},{1,49},{2,50},{3,51},{4,52},{5,53},{6,54},{7,55},{8,56},{9,... | collective-permute-start | bytes 49160 | tf_op jit(solution)/shard_map/ppermute | solution.py:368
  112.3 1.4 collective-permute-start.13
  113.6 3.8 %collective-permute-start.12 = (f32[4,4,2,1,128]{4,2,1,0,3:T(2,128)S(1)}, f32[4,4,2,1,128]{4,2,1,0,3:T(2,128)S(1)}, u32[]{:S(2)}, u32[]{:S(2)}) collective-permute-start(f32[4,4,2,1,128]{4,2,1,0,3:T(2,128)S(1)} %get-tuple-element.63), channel_id=1, source_target_pairs={{0,16},{1,17},{2,18},{3,19},{4,20},{5,21},{6,22},{7,23},{8,24},{9,... | collective-permute-start | bytes 49160 | tf_op jit(solution)/shard_map/ppermute | solution.py:368
  117.5 1.3 collective-permute-start.15
  124.9 3.8 %collective-permute-start.16 = (bf16[2048,128]{1,0:T(8,128)(2,1)S(1)}, bf16[2048,128]{1,0:T(8,128)(2,1)S(1)}, u32[]{:S(2)}, u32[]{:S(2)}) collective-permute-start(bf16[2048,128]{1,0:T(8,128)(2,1)S(1)} %get-tuple-element.40), channel_id=1, source_target_pairs={{0,128},{128,0},{1,129},{129,1},{2,130},{130,2},{3,131},{131,3},{4... | collective-permute-start | bytes 1572872 | tf_op jit(solution)/shard_map/ppermute | solution.py:351
  126.0 3.6 %collective-permute-start.18 = (bf16[1024,128]{1,0:T(8,128)(2,1)}, bf16[1024,128]{1,0:T(8,128)(2,1)}, u32[]{:S(2)}, u32[]{:S(2)}) collective-permute-start(bf16[1024,128]{1,0:T(8,128)(2,1)} %get-tuple-element.65), channel_id=1, source_target_pairs={{128,140},{129,141},{130,142},{131,143},{132,136},{133,137},{134,1... | collective-permute-start | bytes 786440 | tf_op jit(solution)/shard_map/ppermute | solution.py:368
  127.4 2.3 collective-permute-start.19
  129.6 6.7 %collective-permute-start.17 = (bf16[1024,128]{1,0:T(8,128)(2,1)}, bf16[1024,128]{1,0:T(8,128)(2,1)}, u32[]{:S(2)}, u32[]{:S(2)}) collective-permute-start(bf16[1024,128]{1,0:T(8,128)(2,1)} %slice.307), channel_id=1, source_target_pairs={{0,16},{1,17},{2,18},{3,19},{4,20},{5,21},{6,22},{7,23},{8,24},{9,... | collective-permute-start | bytes 786440 | tf_op jit(solution)/shard_map/ppermute | solution.py:368
  137.6 10.6 %collective-permute-start.22 = (bf16[256,128]{1,0:T(8,128)(2,1)S(1)}, bf16[256,128]{1,0:T(8,128)(2,1)S(1)}, u32[]{:S(2)}, u32[]{:S(2)}) collective-permute-start(bf16[256,128]{1,0:T(8,128)(2,1)S(1)} %get-tuple-element.73), channel_id=1, source_target_pairs={{0,64},{1,65},{2,66},{3,67},{4,68},{5,69},{6,70},{7,71},{8,72},{9,... | collective-permute-start | bytes 196616 | tf_op jit(solution)/shard_map/ppermute | solution.py:368
  139.8 8.3 %collective-permute-start.21 = (bf16[256,128]{1,0:T(8,128)(2,1)S(1)}, bf16[256,128]{1,0:T(8,128)(2,1)S(1)}, u32[]{:S(2)}, u32[]{:S(2)}) collective-permute-start(bf16[256,128]{1,0:T(8,128)(2,1)S(1)} %get-tuple-element.74), channel_id=1, source_target_pairs={{0,112},{1,113},{2,114},{3,115},{4,116},{5,117},{6,118},{7,119},{8... | collective-permute-start | bytes 196616 | tf_op jit(solution)/shard_map/ppermute | solution.py:368
  142.0 6.6 %collective-permute-start.20 = (bf16[256,128]{1,0:T(8,128)(2,1)S(1)}, bf16[256,128]{1,0:T(8,128)(2,1)S(1)}, u32[]{:S(2)}, u32[]{:S(2)}) collective-permute-start(bf16[256,128]{1,0:T(8,128)(2,1)S(1)} %get-tuple-element.75), channel_id=1, source_target_pairs={{0,48},{1,49},{2,50},{3,51},{4,52},{5,53},{6,54},{7,55},{8,56},{9,... | collective-permute-start | bytes 196616 | tf_op jit(solution)/shard_map/ppermute | solution.py:368
  152.8 10.7 %collective-permute-start.23 = (bf16[64,40,128]{2,1,0:T(8,128)(2,1)S(1)}, bf16[64,40,128]{2,1,0:T(8,128)(2,1)S(1)}, u32[]{:S(2)}, u32[]{:S(2)}) collective-permute-start(bf16[64,40,128]{2,1,0:T(8,128)(2,1)S(1)} %get-tuple-element.50), channel_id=1, source_target_pairs={{0,1},{1,0},{2,3},{3,2},{4,5},{5,4},{6,7},{7,6},{8,9},{9,8},{10,11... | collective-permute-start | bytes 1966088 | tf_op jit(solution)/shard_map/ppermute | solution.py:388
  154.3 10.6 %collective-permute-start.26 = (bf16[64,40,128]{2,1,0:T(8,128)(2,1)S(1)}, bf16[64,40,128]{2,1,0:T(8,128)(2,1)S(1)}, u32[]{:S(2)}, u32[]{:S(2)}) collective-permute-start(bf16[64,40,128]{2,1,0:T(8,128)(2,1)S(1)} %get-tuple-element.52), channel_id=1, source_target_pairs={{0,4},{1,5},{2,6},{3,7},{4,0},{5,1},{6,2},{7,3},{8,12},{9,13},{10,... | collective-permute-start | bytes 1966088 | tf_op jit(solution)/shard_map/ppermute | solution.py:388
  154.8 11.0 %collective-permute-start.29 = (bf16[64,40,128]{2,1,0:T(8,128)(2,1)S(1)}, bf16[64,40,128]{2,1,0:T(8,128)(2,1)S(1)}, u32[]{:S(2)}, u32[]{:S(2)}) collective-permute-start(bf16[64,40,128]{2,1,0:T(8,128)(2,1)S(1)} %get-tuple-element.54), channel_id=1, source_target_pairs={{0,16},{1,17},{2,18},{3,19},{4,20},{5,21},{6,22},{7,23},{8,24},{9,... | collective-permute-start | bytes 1966088 | tf_op jit(solution)/shard_map/ppermute | solution.py:388
  163.7 7.2 %collective-permute-start.24 = (bf16[32,40,128]{2,1,0:T(8,128)(2,1)S(1)}, bf16[32,40,128]{2,1,0:T(8,128)(2,1)S(1)}, u32[]{:S(2)}, u32[]{:S(2)}) collective-permute-start(bf16[32,40,128]{2,1,0:T(8,128)(2,1)S(1)} %slice.306), channel_id=1, source_target_pairs={{0,4},{1,5},{2,6},{3,7},{4,0},{5,1},{6,2},{7,3},{8,12},{9,13},{10,... | collective-permute-start | bytes 983048 | tf_op jit(solution)/shard_map/ppermute | solution.py:388
  165.1 7.2 %collective-permute-start.27 = (bf16[32,40,128]{2,1,0:T(8,128)(2,1)S(1)}, bf16[32,40,128]{2,1,0:T(8,128)(2,1)S(1)}, u32[]{:S(2)}, u32[]{:S(2)}) collective-permute-start(bf16[32,40,128]{2,1,0:T(8,128)(2,1)S(1)} %slice.305), channel_id=1, source_target_pairs={{0,16},{1,17},{2,18},{3,19},{4,20},{5,21},{6,22},{7,23},{8,24},{9,... | collective-permute-start | bytes 983048 | tf_op jit(solution)/shard_map/ppermute | solution.py:388
  166.0 7.3 %collective-permute-start.30 = (bf16[32,40,128]{2,1,0:T(8,128)(2,1)S(1)}, bf16[32,40,128]{2,1,0:T(8,128)(2,1)S(1)}, u32[]{:S(2)}, u32[]{:S(2)}) collective-permute-start(bf16[32,40,128]{2,1,0:T(8,128)(2,1)S(1)} %slice.304), channel_id=1, source_target_pairs={{0,1},{1,0},{2,3},{3,2},{4,5},{5,4},{6,7},{7,6},{8,9},{9,8},{10,11... | collective-permute-start | bytes 983048 | tf_op jit(solution)/shard_map/ppermute | solution.py:388
  170.9 5.4 %collective-permute-start.25 = (bf16[16,40,128]{2,1,0:T(8,128)(2,1)S(1)}, bf16[16,40,128]{2,1,0:T(8,128)(2,1)S(1)}, u32[]{:S(2)}, u32[]{:S(2)}) collective-permute-start(bf16[16,40,128]{2,1,0:T(8,128)(2,1)S(1)} %slice.310), channel_id=1, source_target_pairs={{0,16},{1,17},{2,18},{3,19},{4,20},{5,21},{6,22},{7,23},{8,24},{9,... | collective-permute-start | bytes 491528 | tf_op jit(solution)/shard_map/ppermute | solution.py:388
  172.3 5.4 %collective-permute-start.28 = (bf16[16,40,128]{2,1,0:T(8,128)(2,1)S(1)}, bf16[16,40,128]{2,1,0:T(8,128)(2,1)S(1)}, u32[]{:S(2)}, u32[]{:S(2)}) collective-permute-start(bf16[16,40,128]{2,1,0:T(8,128)(2,1)S(1)} %slice.309), channel_id=1, source_target_pairs={{0,1},{1,0},{2,3},{3,2},{4,5},{5,4},{6,7},{7,6},{8,9},{9,8},{10,11... | collective-permute-start | bytes 491528 | tf_op jit(solution)/shard_map/ppermute | solution.py:388
  173.4 5.4 %collective-permute-start.31 = (bf16[16,40,128]{2,1,0:T(8,128)(2,1)S(1)}, bf16[16,40,128]{2,1,0:T(8,128)(2,1)S(1)}, u32[]{:S(2)}, u32[]{:S(2)}) collective-permute-start(bf16[16,40,128]{2,1,0:T(8,128)(2,1)S(1)} %slice.308), channel_id=1, source_target_pairs={{0,4},{1,5},{2,6},{3,7},{4,0},{5,1},{6,2},{7,3},{8,12},{9,13},{10,... | collective-permute-start | bytes 491528 | tf_op jit(solution)/shard_map/ppermute | solution.py:388
  178.9 6.2 %collective-permute-start.32 = (bf16[3,4,40,128]{3,2,1,0:T(8,128)(2,1)S(1)}, bf16[3,4,40,128]{3,2,1,0:T(8,128)(2,1)S(1)}, u32[]{:S(2)}, u32[]{:S(2)}) collective-permute-start(bf16[3,4,40,128]{3,2,1,0:T(8,128)(2,1)S(1)} %get-tuple-element.70), channel_id=1, source_target_pairs={{0,12},{1,13},{2,14},{3,15},{4,8},{5,9},{6,10},{7,11},{8,4},{9,5},... | collective-permute-start | bytes 368648 | tf_op jit(solution)/shard_map/ppermute | solution.py:388
  180.6 7.0 %collective-permute-start.34 = (bf16[3,4,40,128]{3,2,1,0:T(8,128)(2,1)S(1)}, bf16[3,4,40,128]{3,2,1,0:T(8,128)(2,1)S(1)}, u32[]{:S(2)}, u32[]{:S(2)}) collective-permute-start(bf16[3,4,40,128]{3,2,1,0:T(8,128)(2,1)S(1)} %get-tuple-element.71), channel_id=1, source_target_pairs={{0,15},{1,14},{2,13},{3,12},{4,11},{5,10},{6,9},{7,8},{8,7},{9,6},... | collective-permute-start | bytes 368648 | tf_op jit(solution)/shard_map/ppermute | solution.py:388
  182.8 5.1 %collective-permute-start.33 = (bf16[3,4,40,128]{3,2,1,0:T(8,128)(2,1)S(1)}, bf16[3,4,40,128]{3,2,1,0:T(8,128)(2,1)S(1)}, u32[]{:S(2)}, u32[]{:S(2)}) collective-permute-start(bf16[3,4,40,128]{3,2,1,0:T(8,128)(2,1)S(1)} %get-tuple-element.72), channel_id=1, source_target_pairs={{0,3},{1,2},{2,1},{3,0},{4,7},{5,6},{6,5},{7,4},{8,11},{9,10},{10,... | collective-permute-start | bytes 368648 | tf_op jit(solution)/shard_map/ppermute | solution.py:388
  187.9 6.3 %collective-permute-start.35 = (bf16[3,4,40,128]{3,2,1,0:T(8,128)(2,1)S(1)}, bf16[3,4,40,128]{3,2,1,0:T(8,128)(2,1)S(1)}, u32[]{:S(2)}, u32[]{:S(2)}) collective-permute-start(bf16[3,4,40,128]{3,2,1,0:T(8,128)(2,1)S(1)} %fusion.5), channel_id=1, source_target_pairs={{0,112},{1,113},{2,114},{3,115},{4,116},{5,117},{6,118},{7,119},{8... | collective-permute-start | bytes 368648 | tf_op jit(solution)/shard_map/ppermute | solution.py:388
  194.3 7.1 %collective-permute-start.36 = (bf16[3,4,40,128]{3,2,1,0:T(8,128)(2,1)S(1)}, bf16[3,4,40,128]{3,2,1,0:T(8,128)(2,1)S(1)}, u32[]{:S(2)}, u32[]{:S(2)}) collective-permute-start(bf16[3,4,40,128]{3,2,1,0:T(8,128)(2,1)S(1)} %bitcast.86), channel_id=1, source_target_pairs={{0,48},{1,49},{2,50},{3,51},{4,52},{5,53},{6,54},{7,55},{8,56},{9,... | collective-permute-start | bytes 368648 | tf_op jit(solution)/shard_map/ppermute | solution.py:388
  201.4 7.1 %collective-permute-start.39 = (bf16[3,4,40,128]{3,2,1,0:T(8,128)(2,1)S(1)}, bf16[3,4,40,128]{3,2,1,0:T(8,128)(2,1)S(1)}, u32[]{:S(2)}, u32[]{:S(2)}) collective-permute-start(bf16[3,4,40,128]{3,2,1,0:T(8,128)(2,1)S(1)} %bitcast.81), channel_id=1, source_target_pairs={{0,15},{1,14},{2,13},{3,12},{4,11},{5,10},{6,9},{7,8},{8,7},{9,6},... | collective-permute-start | bytes 368648 | tf_op jit(solution)/shard_map/ppermute | solution.py:388
  205.3 5.6 %collective-permute-start.38 = (bf16[3,4,40,128]{3,2,1,0:T(8,128)(2,1)S(1)}, bf16[3,4,40,128]{3,2,1,0:T(8,128)(2,1)S(1)}, u32[]{:S(2)}, u32[]{:S(2)}) collective-permute-start(bf16[3,4,40,128]{3,2,1,0:T(8,128)(2,1)S(1)} %bitcast.82), channel_id=1, source_target_pairs={{0,3},{1,2},{2,1},{3,0},{4,7},{5,6},{6,5},{7,4},{8,11},{9,10},{10,... | collective-permute-start | bytes 368648 | tf_op jit(solution)/shard_map/ppermute | solution.py:388
  205.3 7.1 %collective-permute-start.37 = (bf16[3,4,40,128]{3,2,1,0:T(8,128)(2,1)S(1)}, bf16[3,4,40,128]{3,2,1,0:T(8,128)(2,1)S(1)}, u32[]{:S(2)}, u32[]{:S(2)}) collective-permute-start(bf16[3,4,40,128]{3,2,1,0:T(8,128)(2,1)S(1)} %bitcast.83), channel_id=1, source_target_pairs={{0,12},{1,13},{2,14},{3,15},{4,8},{5,9},{6,10},{7,11},{8,4},{9,5},... | collective-permute-start | bytes 368648 | tf_op jit(solution)/shard_map/ppermute | solution.py:388
  212.5 7.0 %collective-permute-start.40 = (bf16[16,40,128]{2,1,0:T(8,128)(2,1)S(1)}, bf16[16,40,128]{2,1,0:T(8,128)(2,1)S(1)}, u32[]{:S(2)}, u32[]{:S(2)}) collective-permute-start(bf16[16,40,128]{2,1,0:T(8,128)(2,1)S(1)} %get-tuple-element.69), channel_id=1, source_target_pairs={{0,16},{1,17},{2,18},{3,19},{4,20},{5,21},{6,22},{7,23},{8,24},{9,... | collective-permute-start | bytes 491528 | tf_op jit(solution)/shard_map/ppermute | solution.py:388
  215.5 7.3 %collective-permute-start.43 = (bf16[16,40,128]{2,1,0:T(8,128)(2,1)S(1)}, bf16[16,40,128]{2,1,0:T(8,128)(2,1)S(1)}, u32[]{:S(2)}, u32[]{:S(2)}) collective-permute-start(bf16[16,40,128]{2,1,0:T(8,128)(2,1)S(1)} %get-tuple-element.68), channel_id=1, source_target_pairs={{0,1},{1,0},{2,3},{3,2},{4,5},{5,4},{6,7},{7,6},{8,9},{9,8},{10,11... | collective-permute-start | bytes 491528 | tf_op jit(solution)/shard_map/ppermute | solution.py:388
  219.5 5.3 %collective-permute-start.46 = (bf16[16,40,128]{2,1,0:T(8,128)(2,1)S(1)}, bf16[16,40,128]{2,1,0:T(8,128)(2,1)S(1)}, u32[]{:S(2)}, u32[]{:S(2)}) collective-permute-start(bf16[16,40,128]{2,1,0:T(8,128)(2,1)S(1)} %get-tuple-element.67), channel_id=1, source_target_pairs={{0,4},{1,5},{2,6},{3,7},{4,0},{5,1},{6,2},{7,3},{8,12},{9,13},{10,... | collective-permute-start | bytes 491528 | tf_op jit(solution)/shard_map/ppermute | solution.py:388
  219.5 8.8 %collective-permute-start.41 = (bf16[32,40,128]{2,1,0:T(8,128)(2,1)S(1)}, bf16[32,40,128]{2,1,0:T(8,128)(2,1)S(1)}, u32[]{:S(2)}, u32[]{:S(2)}) collective-permute-start(bf16[32,40,128]{2,1,0:T(8,128)(2,1)S(1)} %pad_maximum_fusion.5), channel_id=1, source_target_pairs={{0,4},{1,5},{2,6},{3,7},{4,0},{5,1},{6,2},{7,3},{8,12},{9,13},{10,... | collective-permute-start | bytes 983048 | tf_op jit(solution)/shard_map/ppermute | solution.py:388
  222.8 7.9 %collective-permute-start.44 = (bf16[32,40,128]{2,1,0:T(8,128)(2,1)S(1)}, bf16[32,40,128]{2,1,0:T(8,128)(2,1)S(1)}, u32[]{:S(2)}, u32[]{:S(2)}) collective-permute-start(bf16[32,40,128]{2,1,0:T(8,128)(2,1)S(1)} %pad_maximum_fusion.6), channel_id=1, source_target_pairs={{0,16},{1,17},{2,18},{3,19},{4,20},{5,21},{6,22},{7,23},{8,24},{9,... | collective-permute-start | bytes 983048 | tf_op jit(solution)/shard_map/ppermute | solution.py:388
  224.8 7.2 %collective-permute-start.47 = (bf16[32,40,128]{2,1,0:T(8,128)(2,1)S(1)}, bf16[32,40,128]{2,1,0:T(8,128)(2,1)S(1)}, u32[]{:S(2)}, u32[]{:S(2)}) collective-permute-start(bf16[32,40,128]{2,1,0:T(8,128)(2,1)S(1)} %pad_maximum_fusion.7), channel_id=1, source_target_pairs={{0,1},{1,0},{2,3},{3,2},{4,5},{5,4},{6,7},{7,6},{8,9},{9,8},{10,11... | collective-permute-start | bytes 983048 | tf_op jit(solution)/shard_map/ppermute | solution.py:388
  228.4 10.9 %collective-permute-start.42 = (bf16[64,40,128]{2,1,0:T(8,128)(2,1)S(1)}, bf16[64,40,128]{2,1,0:T(8,128)(2,1)S(1)}, u32[]{:S(2)}, u32[]{:S(2)}) collective-permute-start(bf16[64,40,128]{2,1,0:T(8,128)(2,1)S(1)} %pad_maximum_fusion.1.rest_0_), channel_id=1, source_target_pairs={{0,1},{1,0},{2,3},{3,2},{4,5},{5,4},{6,7},{7,6},{8,9},{9,8},{10,11... | collective-permute-start | bytes 1966088 | tf_op jit(solution)/shard_map/ppermute | solution.py:388
  230.8 10.7 %collective-permute-start.45 = (bf16[64,40,128]{2,1,0:T(8,128)(2,1)S(1)}, bf16[64,40,128]{2,1,0:T(8,128)(2,1)S(1)}, u32[]{:S(2)}, u32[]{:S(2)}) collective-permute-start(bf16[64,40,128]{2,1,0:T(8,128)(2,1)S(1)} %pad_maximum_fusion.2.rest_1_), channel_id=1, source_target_pairs={{0,4},{1,5},{2,6},{3,7},{4,0},{5,1},{6,2},{7,3},{8,12},{9,13},{10,... | collective-permute-start | bytes 1966088 | tf_op jit(solution)/shard_map/ppermute | solution.py:388
  232.0 10.7 %collective-permute-start.48 = (bf16[64,40,128]{2,1,0:T(8,128)(2,1)S(1)}, bf16[64,40,128]{2,1,0:T(8,128)(2,1)S(1)}, u32[]{:S(2)}, u32[]{:S(2)}) collective-permute-start(bf16[64,40,128]{2,1,0:T(8,128)(2,1)S(1)} %pad_maximum_fusion.3.rest_2_), channel_id=1, source_target_pairs={{0,16},{1,17},{2,18},{3,19},{4,20},{5,21},{6,22},{7,23},{8,24},{9,... | collective-permute-start | bytes 1966088 | tf_op jit(solution)/shard_map/ppermute | solution.py:388
  (8 other events, 41.0 us)
where the time goes:
time: 249 us; the launch traced here: 246 us
  waiting for transfers between devices  74.6 us (30%)
  starting transfers between devices  74.3 us (30%)
  blocking collectives  57.6 us (23%)
  Pallas kernels  29.9 us (12%)
  local copies, waits for them, and re-layouts  5.4 us (2%)
  other arithmetic  2.83 us (1%)
    all_to_all x2, blocking collectives, exchange(): return lax.all_to_all(value, axes, split_axis=0, concat_axis=0, tiled=True)  57.6 us
    ppermute x26, waiting for transfers between devices, trade(): return lax.ppermute(value, AXES, pairs)  48.5 us
    ppermute x26, starting transfers between devices, trade(): return lax.ppermute(value, AXES, pairs)  36.5 us
    ppermute x18, starting transfers between devices, across(): return lax.ppermute(value, AXES, pairs)  25.7 us
    ppermute x18, waiting for transfers between devices, across(): return lax.ppermute(value, AXES, pairs)  23 us
    ppermute x5, starting transfers between devices, swap(): return lax.ppermute(value, 'side', [(0, 1), (1, 0)])  12.1 us
    pallas_call x2, Pallas kernels, finish(): pl.pallas_call(functools.partial(finish_kernel, parts, half), out_shape=[...  6.2 us
    pallas_call x1, Pallas kernels, on_device(): call(grad_kernel, [((UROWS, EMB), F32), ((UROWS, EMB), BF16), ((ICOLS, EM...  6.14 us
  transfers between devices with their start and end apart: 49, of which 32 were waited for; matrix products, arithmetic and copies ran while one was open for 2% of the time, Pallas kernels for 2%

commit v1 on v0

--- a/solution.py
+++ b/solution.py
@@ -210,7 +210,8 @@
 
 
 def grad_kernel(side_ref, *refs):
-    total_ref, sent_ref, keep_ref, send_ref, away_ref, grad_ref, turned_ref = refs[6:]
+    total_ref, sent_ref, *outs, grad_ref, turned_ref = refs[6:]
+    keep_refs, send_refs, away_refs = outs[0:2], outs[2:4], outs[4:6]
     users, items = choose(side_ref, refs[:6])
     first = side_ref[0] == 0
     col = [jnp.where(first, sent_ref[k], total_ref[LROWS + k]) for k in range(LROWS)]
@@ -227,17 +228,18 @@
             eye = jnp.where(iota((TOK, TOK), 0) == iota((TOK, TOK), 1), own, 0.0)
             grad_ref[:, 0:TOK] = grad_ref[:, 0:TOK] - eye
         grad = grad_ref[...].astype(BF16)
-        keep_ref[c * CHUNK:(c + 1) * CHUNK, :] = dot(grad, items, NN) * GRAD_SCALE
+        rows = slice(c * CHUNK % QUART, c * CHUNK % QUART + CHUNK)
+        keep_refs[c * CHUNK // QUART][rows, :] = dot(grad, items, NN) * GRAD_SCALE
         term = dot(chunk, grad, TN)
         if c == 0:
             turned_ref[...] = term
         else:
             turned_ref[...] += term
     for c in range(NZ):
-        rows = slice(c * CHUNK, (c + 1) * CHUNK)
-        of_items = (turned_ref[:, rows].T * GRAD_SCALE).astype(BF16)
-        away_ref[rows, :] = of_items
-        send_ref[rows, :] = jnp.where(first, of_items, keep_ref[rows, :].astype(BF16))
+        half, rows = c * CHUNK // QUART, slice(c * CHUNK % QUART, c * CHUNK % QUART + CHUNK)
+        of_items = (turned_ref[:, c * CHUNK:(c + 1) * CHUNK].T * GRAD_SCALE).astype(BF16)
+        away_refs[half][rows, :] = of_items
+        send_refs[half][rows, :] = jnp.where(first, of_items, keep_refs[half][rows, :].astype(BF16))
 
 
 def piece_at(part, slot, code):
@@ -509,17 +511,20 @@
     )(side, *pieces)
     sums = sum_all(*sums, side[0])
 
-    keep, send, away = call(
+    *keep, send_near, send_far, away_two, away_three = call(
         grad_kernel,
-        [((UROWS, EMB), F32), ((UROWS, EMB), BF16), ((ICOLS, EMB), BF16)],
+        [((QUART, EMB), F32)] * 2 + [((QUART, EMB), BF16)] * 4,
         [SMEM] + [VMEM] * 8,
         [pltpu.VMEM((CHUNK, ICOLS), F32), pltpu.VMEM((EMB, ICOLS), F32)],
         mib=32,
     )(side, *pieces, *sums)
-    got = [across(away[(d - 2) * QUART:(d - 1) * QUART], None, {"y": d}) for d in (2, 3)]
-    grad = jnp.where(side[0] == 0, keep, 0.0) + swap(send).astype(F32)
-    got.append(across(grad[QUART:].astype(BF16), {"z": 1}, {"y": 1}))
-    grad = grad[:QUART] + got[2].astype(F32) + got[0].astype(F32) + got[1].astype(F32)
+    got = [across(away_two, None, {"y": 2}), across(away_three, None, {"y": 3})]
+    near, far = [
+        jnp.where(side[0] == 0, mine, 0.0) + swap(send).astype(F32)
+        for mine, send in zip(keep, (send_near, send_far))
+    ]
+    got.append(across(far.astype(BF16), {"z": 1}, {"y": 1}))
+    grad = near + got[2].astype(F32) + got[0].astype(F32) + got[1].astype(F32)
     grad = grad.reshape(4, TOK, EMB)
     got = [across(grad[d + 1].astype(BF16), *flips) for d, flips in enumerate(FOURS)]
 
@@ -541,7 +546,8 @@
     )(place, grad[0], *got, u, r, x, *slopes, weight_mid, weight_out)
     pairs = spread_weights(sum_weights(sums[:PARTS], sums[PARTS:]))
     grads = finish(tuple(range(PARTS)), 0, place, pairs[0::2], ())
-    grads = finish(tuple(range(PARTS)), 1, place, pairs[1::2], grads)
+    grads = finish((0,), 1, place, pairs[1:2], grads)
+    grads = finish(tuple(range(1, PARTS)), 1, place, pairs[3::2], grads)
     return tuple(g[None] for g in grads)
 
 

time: 249 us -> 248 us (level)
  starting transfers between devices: 74.3 us -> 68.9 us
  waiting for transfers between devices: 74.6 us -> 79 us
  local copies, waits for them, and re-layouts: 5.4 us -> 2.42 us
    ppermute x26, starting transfers between devices: 36.5 us -> 30.5 us  [trade(): return lax.ppermute(value, AXES, pairs)]
    ppermute x26, waiting for transfers between devices: 48.5 us -> 51.5 us  [trade(): return lax.ppermute(value, AXES, pairs)]
    pallas_call x2 -> x3, Pallas kernels: 6.2 us -> 7.45 us  [finish(): pl.pallas_call(functools.partial(finish_kernel, parts, half), out_shape=[...]
    ppermute x5 -> x6, starting transfers between devices: 12.1 us -> 12.7 us  [swap(): return lax.ppermute(value, 'side', [(0, 1), (1, 0)])]
  transfers between devices with their start and end apart: 49 -> 50, of which waited for: 32 -> 31; matrix products, arithmetic and copies ran while one was open for 2% -> 1% of each run, Pallas kernels for 2% -> 3%
where the time goes in v1:
time: 248 us; the launch traced here: 244 us
  waiting for transfers between devices  79 us (32%)
  starting transfers between devices  68.9 us (28%)
  blocking collectives  57.6 us (23%)
  Pallas kernels  31.2 us (13%)
  other arithmetic  3.73 us (2%)
    all_to_all x2, blocking collectives, exchange(): return lax.all_to_all(value, axes, split_axis=0, concat_axis=0, tiled=True)  57.6 us
    ppermute x26, waiting for transfers between devices, trade(): return lax.ppermute(value, AXES, pairs)  51.5 us
    ppermute x26, starting transfers between devices, trade(): return lax.ppermute(value, AXES, pairs)  30.5 us
    ppermute x18, starting transfers between devices, across(): return lax.ppermute(value, AXES, pairs)  25.7 us
    ppermute x18, waiting for transfers between devices, across(): return lax.ppermute(value, AXES, pairs)  24.4 us
    ppermute x6, starting transfers between devices, swap(): return lax.ppermute(value, 'side', [(0, 1), (1, 0)])  12.7 us
    pallas_call x3, Pallas kernels, finish(): pl.pallas_call(functools.partial(finish_kernel, parts, half), out_shape=[...  7.45 us
    pallas_call x1, Pallas kernels, on_device(): call(grad_kernel, [((QUART, EMB), F32)] * 2 + [((QUART, EMB), BF16)] * 4,...  6.14 us
  transfers between devices with their start and end apart: 50, of which 31 were waited for; matrix products, arithmetic and copies ran while one was open for 1% of the time, Pallas kernels for 3%

profile of v1, /device:TPU:2, one launch (start us, length us, event | category | flops | bytes accessed | tf_op | source)
XLA Modules:
  0.0 244.1 jit_solution(2776178337019311823)
XLA Ops:
  0.6 1.6 shard_map.85
  2.3 26.7 %all_to_all.10 = s32[128,1,128]{2,1,0:T(1,128)S(1)} all-to-all(s32[128,1,128]{2,1,0:T(1,128)} %bitcast.95), channel_id=1, replica_groups=mesh['side'=2,'z'=8,'y'=4,'x'=4] {'z','y','x'}, dimensions={0} | all-to-all | bytes 131072 | tf_op jit(solution)/shard_map/all_to_all | solution.py:349
  30.1 2.0 shard_map.86
  32.1 30.9 %all_to_all.11 = bf16[128,8,384]{2,1,0:T(8,128)(2,1)} all-to-all(bf16[128,8,384]{2,1,0:T(8,128)(2,1)S(1)} %bitcast.66), channel_id=1, replica_groups=mesh['side'=2,'z'=8,'y'=4,'x'=4] {'z','y','x'}, dimensions={0} | all-to-all | bytes 1572864 | tf_op jit(solution)/shard_map/all_to_all | solution.py:349
  63.0 5.1 %shard_map.87 = (bf16[256,768]{1,0:T(8,128)(2,1)}, f32[256,128]{1,0:T(8,128)}, f32[256,128]{1,0:T(8,128)}, bf16[256,128]{1,0:T(8,128)(2,1)}) custom-call(s32[1,256]{1,0:T(1,128)} %get-tuple-element.38.position_ref, bf16[1024,384]{1,0:T(8,128)(2,1)} %bitcast.73, bf16[768,1024]{1,0:T(8,128)(2,1)} %bitcast.64, bf16[1024,1024]{1,0:T(8,128)(2,1)} %bitcast.61, ...), custom_call_target="tpu_custom_call" | custom-call | tf_op jit(solution)/shard_map/pallas_call | solution.py:494
  68.2 3.4 %collective-permute-start.1 = (bf16[256,128]{1,0:T(8,128)(2,1)}, bf16[256,128]{1,0:T(8,128)(2,1)S(1)}, u32[]{:S(2)}, u32[]{:S(2)}) collective-permute-start(bf16[256,128]{1,0:T(8,128)(2,1)} %get-tuple-element.40), channel_id=1, source_target_pairs={{0,112},{1,113},{2,114},{3,115},{4,116},{5,117},{6,118},{7,119},{8... | collective-permute-start | bytes 196616 | tf_op jit(solution)/shard_map/ppermute | solution.py:370
  71.6 3.1 %collective-permute-start = (bf16[256,128]{1,0:T(8,128)(2,1)}, bf16[256,128]{1,0:T(8,128)(2,1)S(1)}, u32[]{:S(2)}, u32[]{:S(2)}) collective-permute-start(bf16[256,128]{1,0:T(8,128)(2,1)} %get-tuple-element.40), channel_id=1, source_target_pairs={{0,48},{1,49},{2,50},{3,51},{4,52},{5,53},{6,54},{7,55},{8,56},{9,... | collective-permute-start | bytes 196616 | tf_op jit(solution)/shard_map/ppermute | solution.py:370
  75.6 3.4 %collective-permute-done = bf16[256,128]{1,0:T(8,128)(2,1)S(1)} collective-permute-done((bf16[256,128]{1,0:T(8,128)(2,1)}, bf16[256,128]{1,0:T(8,128)(2,1)S(1)}, u32[]{:S(2)}, u32[]{:S(2)}) %collective-permute-start) | collective-permute-done | bytes 65568 | tf_op jit(solution)/shard_map/ppermute | solution.py:370
  80.5 5.0 %collective-permute-done.3.refs_1_ = bf16[1024,128]{1,0:T(8,128)(2,1)S(1)} collective-permute-done((bf16[1024,128]{1,0:T(8,128)(2,1)S(1)}, bf16[1024,128]{1,0:T(8,128)(2,1)S(1)}, u32[]{:S(2)}, u32[]{:S(2)}) %collective-permute-start.3) | collective-permute-done | bytes 262176 | tf_op jit(solution)/shard_map/ppermute | solution.py:370
  85.5 11.5 %collective-permute-start.7 = (bf16[1024,128]{1,0:T(8,128)(2,1)S(1)}, bf16[1024,128]{1,0:T(8,128)(2,1)S(1)}, u32[]{:S(2)}, u32[]{:S(2)}) collective-permute-start(bf16[1024,128]{1,0:T(8,128)(2,1)S(1)} %collective-permute-done.3.refs_1_), channel_id=1, source_target_pairs={{0,128},{128,0},{1,129},{129,1},{2,130},{130,2},{3,131},{131,3},{4... | collective-permute-start | bytes 786440 | tf_op jit(solution)/shard_map/ppermute | solution.py:353
  98.2 2.6 %shard_map.88 = (f32[16,1,128]{2,1,0:T(1,128)S(1)}, f32[16,1,128]{2,1,0:T(1,128)S(1)}) custom-call(s32[1]{0:T(128)} %bitcast.3.side_ref, bf16[1024,128]{1,0:T(8,128)(2,1)S(1)} %constant_dynamic-update-slice_fusion.refs_0_, bf16[1024,128]{1,0:T(8,128)(2,1)S(1)} %collective-permute-done.3.refs_1_, bf16[1024,128]{1,0:T(8,128)(2,1)S(1)} %collective-permute-done.4.refs_2_, ...), custom_call_target="tpu_custom_call" | custom-call | tf_op jit(solution)/shard_map/pallas_call | solution.py:509
  102.2 4.8 %collective-permute-start.11 = (f32[4,4,2,1,128]{4,2,1,0,3:T(2,128)S(1)}, f32[4,4,2,1,128]{4,2,1,0,3:T(2,128)S(1)}, u32[]{:S(2)}, u32[]{:S(2)}) collective-permute-start(f32[4,4,2,1,128]{4,2,1,0,3:T(2,128)S(1)} %bitcast.92), channel_id=1, source_target_pairs={{0,64},{1,65},{2,66},{3,67},{4,68},{5,69},{6,70},{7,71},{8,72},{9,... | collective-permute-start | bytes 49160 | tf_op jit(solution)/shard_map/ppermute | solution.py:370
  107.0 1.7 collective-permute-start.9
  109.9 2.6 %collective-permute-done.9 = f32[4,4,2,1,128]{4,2,1,0,3:T(2,128)S(1)} collective-permute-done((f32[4,4,2,1,128]{4,2,1,0,3:T(2,128)S(1)}, f32[4,4,2,1,128]{4,2,1,0,3:T(2,128)S(1)}, u32[]{:S(2)}, u32[]{:S(2)}) %collective-permute-start.9) | collective-permute-done | bytes 16416 | tf_op jit(solution)/shard_map/ppermute | solution.py:370
  114.1 3.7 %collective-permute-done.12 = f32[4,4,2,1,128]{4,2,1,0,3:T(2,128)S(1)} collective-permute-done((f32[4,4,2,1,128]{4,2,1,0,3:T(2,128)S(1)}, f32[4,4,2,1,128]{4,2,1,0,3:T(2,128)S(1)}, u32[]{:S(2)}, u32[]{:S(2)}) %collective-permute-start.12) | collective-permute-done | bytes 16416 | tf_op jit(solution)/shard_map/ppermute | solution.py:370
  119.1 6.1 %shard_map.89 = (f32[1024,128]{1,0:T(8,128)S(1)}, f32[1024,128]{1,0:T(8,128)S(1)}, bf16[1024,128]{1,0:T(8,128)(2,1)S(1)}, bf16[1024,128]{1,0:T(8,128)(2,1)S(1)},...) custom-call(s32[1]{0:T(128)} %bitcast.3.side_ref, ...), custom_call_target="tpu_custom_call" | custom-call | tf_op jit(solution)/shard_map/pallas_call | solution.py:514
  129.4 6.7 %collective-permute-done.18 = bf16[1024,128]{1,0:T(8,128)(2,1)} collective-permute-done((bf16[1024,128]{1,0:T(8,128)(2,1)}, bf16[1024,128]{1,0:T(8,128)(2,1)}, u32[]{:S(2)}, u32[]{:S(2)}) %collective-permute-start.18) | collective-permute-done | bytes 262176 | tf_op jit(solution)/shard_map/ppermute | solution.py:370
  137.5 2.2 collective-permute-start.23
  139.7 2.2 collective-permute-start.22
  141.9 2.5 %collective-permute-start.21 = (bf16[256,128]{1,0:T(8,128)(2,1)S(1)}, bf16[256,128]{1,0:T(8,128)(2,1)S(1)}, u32[]{:S(2)}, u32[]{:S(2)}) collective-permute-start(bf16[256,128]{1,0:T(8,128)(2,1)S(1)} %get-tuple-element.85), channel_id=1, source_target_pairs={{0,48},{1,49},{2,50},{3,51},{4,52},{5,53},{6,54},{7,55},{8,56},{9,... | collective-permute-start | bytes 196616 | tf_op jit(solution)/shard_map/ppermute | solution.py:370
  144.6 2.1 shard_map.90
  146.7 1.8 collective-permute-done.21.sent0_ref
  148.5 4.2 %shard_map.91 = (bf16[64,40,128]{2,1,0:T(8,128)(2,1)S(1)}, bf16[64,40,128]{2,1,0:T(8,128)(2,1)S(1)}, bf16[64,40,128]{2,1,0:T(8,128)(2,1)S(1)}, bf16[64,40,128]{2...) custom-call(s32[3]{0:T(128)S(1)} %pad_add_fusion.place_ref, ...), custom_call_target="tpu_custom_call" | custom-call | tf_op jit(solution)/shard_map/pallas_call | solution.py:540
  152.7 1.5 collective-permute-start.24
  155.3 8.1 %collective-permute-done.24 = bf16[64,40,128]{2,1,0:T(8,128)(2,1)S(1)} collective-permute-done((bf16[64,40,128]{2,1,0:T(8,128)(2,1)S(1)}, bf16[64,40,128]{2,1,0:T(8,128)(2,1)S(1)}, u32[]{:S(2)}, u32[]{:S(2)}) %collective-permute-start.24) | collective-permute-done | bytes 655392 | tf_op jit(solution)/shard_map/ppermute | solution.py:390
  166.7 4.0 %collective-permute-done.25 = bf16[32,40,128]{2,1,0:T(8,128)(2,1)S(1)} collective-permute-done((bf16[32,40,128]{2,1,0:T(8,128)(2,1)S(1)}, bf16[32,40,128]{2,1,0:T(8,128)(2,1)S(1)}, u32[]{:S(2)}, u32[]{:S(2)}) %collective-permute-start.25) | collective-permute-done | bytes 327712 | tf_op jit(solution)/shard_map/ppermute | solution.py:390
  173.3 1.5 collective-permute-start.32
  178.8 1.5 collective-permute-start.33
  180.3 2.2 collective-permute-start.35
  185.0 2.3 collective-permute-done.35
  187.9 2.0 collective-permute-start.36
  189.8 6.2 %collective-permute-done.36 = bf16[3,4,40,128]{3,2,1,0:T(8,128)(2,1)S(1)} collective-permute-done((bf16[3,4,40,128]{3,2,1,0:T(8,128)(2,1)S(1)}, bf16[3,4,40,128]{3,2,1,0:T(8,128)(2,1)S(1)}, u32[]{:S(2)}, u32[]{:S(2)}) %collective-permute-start.36) | collective-permute-done | bytes 122912 | tf_op jit(solution)/shard_map/ppermute | solution.py:390
  196.8 6.1 %collective-permute-done.37 = bf16[3,4,40,128]{3,2,1,0:T(8,128)(2,1)S(1)} collective-permute-done((bf16[3,4,40,128]{3,2,1,0:T(8,128)(2,1)S(1)}, bf16[3,4,40,128]{3,2,1,0:T(8,128)(2,1)S(1)}, u32[]{:S(2)}, u32[]{:S(2)}) %collective-permute-start.37) | collective-permute-done | bytes 122912 | tf_op jit(solution)/shard_map/ppermute | solution.py:390
  202.9 1.8 collective-permute-start.40
  204.8 2.9 %collective-permute-start.38 = (bf16[3,4,40,128]{3,2,1,0:T(8,128)(2,1)S(1)}, bf16[3,4,40,128]{3,2,1,0:T(8,128)(2,1)S(1)}, u32[]{:S(2)}, u32[]{:S(2)}) collective-permute-start(bf16[3,4,40,128]{3,2,1,0:T(8,128)(2,1)S(1)} %bitcast.83), channel_id=1, source_target_pairs={{0,12},{1,13},{2,14},{3,15},{4,8},{5,9},{6,10},{7,11},{8,4},{9,5},... | collective-permute-start | bytes 368648 | tf_op jit(solution)/shard_map/ppermute | solution.py:390
  207.7 2.5 %collective-permute-done.40 = bf16[3,4,40,128]{3,2,1,0:T(8,128)(2,1)S(1)} collective-permute-done((bf16[3,4,40,128]{3,2,1,0:T(8,128)(2,1)S(1)}, bf16[3,4,40,128]{3,2,1,0:T(8,128)(2,1)S(1)}, u32[]{:S(2)}, u32[]{:S(2)}) %collective-permute-start.40) | collective-permute-done | bytes 122912 | tf_op jit(solution)/shard_map/ppermute | solution.py:390
  210.4 2.3 collective-permute-done.38
  212.8 3.5 %collective-permute-start.41 = (bf16[16,40,128]{2,1,0:T(8,128)(2,1)S(1)}, bf16[16,40,128]{2,1,0:T(8,128)(2,1)S(1)}, u32[]{:S(2)}, u32[]{:S(2)}) collective-permute-start(bf16[16,40,128]{2,1,0:T(8,128)(2,1)S(1)} %get-tuple-element.79), channel_id=1, source_target_pairs={{0,1},{1,0},{2,3},{3,2},{4,5},{5,4},{6,7},{7,6},{8,9},{9,8},{10,11... | collective-permute-start | bytes 491528 | tf_op jit(solution)/shard_map/ppermute | solution.py:390
  216.3 1.5 collective-permute-start.47
  217.8 1.8 collective-permute-done.41
  219.6 1.6 collective-permute-start.42
  223.5 3.2 %collective-permute-done.42 = bf16[32,40,128]{2,1,0:T(8,128)(2,1)S(1)} collective-permute-done((bf16[32,40,128]{2,1,0:T(8,128)(2,1)S(1)}, bf16[32,40,128]{2,1,0:T(8,128)(2,1)S(1)}, u32[]{:S(2)}, u32[]{:S(2)}) %collective-permute-start.42) | collective-permute-done | bytes 327712 | tf_op jit(solution)/shard_map/ppermute | solution.py:390
  227.2 1.6 collective-permute-done.48
  228.9 1.7 collective-permute-start.49
  231.3 3.1 %shard_map.92 = (f32[768,1024]{1,0:T(8,128)}, f32[1024,1024]{1,0:T(8,128)}, f32[1024,128]{1,0:T(8,128)}) custom-call(s32[3]{0:T(128)S(1)} %pad_add_fusion.place_ref, bf16[64,40,128]{2,1,0:T(8,128)(2,1)S(1)} %pad_maximum_fusion.3.rest_0_, bf16[64,40,128]{2,1,0:T(8,128)(2,1)S(1)} %pad_maximum_fusion.1.rest_1_, bf16[64,40,128]{2,1,0:T(8,128)(2,1)S(1)} %pad_maximum_fusion.2.rest_2_), custom_call_target="tpu_custom_call" | custom-call | bytes 5898240 | tf_op jit(solution)/shard_map/pallas_call | solution.py:121
  234.4 5.2 %collective-permute-done.49.rest_0_ = bf16[64,40,128]{2,1,0:T(8,128)(2,1)S(1)} collective-permute-done((bf16[64,40,128]{2,1,0:T(8,128)(2,1)S(1)}, bf16[64,40,128]{2,1,0:T(8,128)(2,1)S(1)}, u32[]{:S(2)}, u32[]{:S(2)}) %collective-permute-start.49) | collective-permute-done | bytes 655392 | tf_op jit(solution)/shard_map/ppermute | solution.py:390
  239.5 1.9 shard_map.93
  241.4 2.5 %shard_map.94 = (f32[768,1024]{1,0:T(8,128)}, f32[1024,1024]{1,0:T(8,128)}, f32[1024,128]{1,0:T(8,128)}) custom-call(s32[3]{0:T(128)S(1)} %pad_add_fusion.place_ref, bf16[64,40,128]{2,1,0:T(8,128)(2,1)S(1)} %collective-permute-done.43.rest_0_, ...), custom_call_target="tpu_custom_call", output_to_operand_aliasing={{0}: (3, {}), {1}: (4, {}), {2}: (5, {})} | custom-call | bytes 3932160 | tf_op jit(solution)/shard_map/pallas_call | solution.py:121
  (128 shorter events, 34.4 us)
Async XLA Ops:
  68.1 10.9 %collective-permute-start.2 = (bf16[256,128]{1,0:T(8,128)(2,1)}, bf16[256,128]{1,0:T(8,128)(2,1)S(1)}, u32[]{:S(2)}, u32[]{:S(2)}) collective-permute-start(bf16[256,128]{1,0:T(8,128)(2,1)} %get-tuple-element.40), channel_id=1, source_target_pairs={{0,64},{1,65},{2,66},{3,67},{4,68},{5,69},{6,70},{7,71},{8,72},{9,... | collective-permute-start | bytes 196616 | tf_op jit(solution)/shard_map/ppermute | solution.py:370
  68.2 10.7 %collective-permute-start.1 = (bf16[256,128]{1,0:T(8,128)(2,1)}, bf16[256,128]{1,0:T(8,128)(2,1)S(1)}, u32[]{:S(2)}, u32[]{:S(2)}) collective-permute-start(bf16[256,128]{1,0:T(8,128)(2,1)} %get-tuple-element.40), channel_id=1, source_target_pairs={{0,112},{1,113},{2,114},{3,115},{4,116},{5,117},{6,118},{7,119},{8... | collective-permute-start | bytes 196616 | tf_op jit(solution)/shard_map/ppermute | solution.py:370
  71.6 7.4 %collective-permute-start = (bf16[256,128]{1,0:T(8,128)(2,1)}, bf16[256,128]{1,0:T(8,128)(2,1)S(1)}, u32[]{:S(2)}, u32[]{:S(2)}) collective-permute-start(bf16[256,128]{1,0:T(8,128)(2,1)} %get-tuple-element.40), channel_id=1, source_target_pairs={{0,48},{1,49},{2,50},{3,51},{4,52},{5,53},{6,54},{7,55},{8,56},{9,... | collective-permute-start | bytes 196616 | tf_op jit(solution)/shard_map/ppermute | solution.py:370
  79.0 6.5 %collective-permute-start.3 = (bf16[1024,128]{1,0:T(8,128)(2,1)S(1)}, bf16[1024,128]{1,0:T(8,128)(2,1)S(1)}, u32[]{:S(2)}, u32[]{:S(2)}) collective-permute-start(bf16[1024,128]{1,0:T(8,128)(2,1)S(1)} %constant_dynamic-update-slice_fusion.refs_0_), channel_id=1, source_target_pairs={{0,16},{1,17},{2,18},{3,19},{4,20},{5,21},{6,22},{7,23},{8,24},{9,... | collective-permute-start | bytes 786440 | tf_op jit(solution)/shard_map/ppermute | solution.py:370
  79.1 17.9 %collective-permute-start.5 = (bf16[1024,128]{1,0:T(8,128)(2,1)S(1)}, bf16[1024,128]{1,0:T(8,128)(2,1)S(1)}, u32[]{:S(2)}, u32[]{:S(2)}) collective-permute-start(bf16[1024,128]{1,0:T(8,128)(2,1)S(1)} %constant_dynamic-update-slice_fusion.refs_0_), channel_id=1, source_target_pairs={{128,136},{129,137},{130,138},{131,139},{132,140},{133,141},{134,1... | collective-permute-start | bytes 786440 | tf_op jit(solution)/shard_map/ppermute | solution.py:370
  79.8 17.2 %collective-permute-start.4 = (bf16[1024,128]{1,0:T(8,128)(2,1)S(1)}, bf16[1024,128]{1,0:T(8,128)(2,1)S(1)}, u32[]{:S(2)}, u32[]{:S(2)}) collective-permute-start(bf16[1024,128]{1,0:T(8,128)(2,1)S(1)} %constant_dynamic-update-slice_fusion.refs_0_), channel_id=1, source_target_pairs={{128,140},{129,141},{130,142},{131,143},{132,136},{133,137},{134,1... | collective-permute-start | bytes 786440 | tf_op jit(solution)/shard_map/ppermute | solution.py:370
  85.5 11.5 %collective-permute-start.6 = (bf16[1024,128]{1,0:T(8,128)(2,1)S(1)}, bf16[1024,128]{1,0:T(8,128)(2,1)S(1)}, u32[]{:S(2)}, u32[]{:S(2)}) collective-permute-start(bf16[1024,128]{1,0:T(8,128)(2,1)S(1)} %constant_dynamic-update-slice_fusion.refs_0_), channel_id=1, source_target_pairs={{0,128},{128,0},{1,129},{129,1},{2,130},{130,2},{3,131},{131,3},{4... | collective-permute-start | bytes 786440 | tf_op jit(solution)/shard_map/ppermute | solution.py:353
  85.5 12.7 %collective-permute-start.7 = (bf16[1024,128]{1,0:T(8,128)(2,1)S(1)}, bf16[1024,128]{1,0:T(8,128)(2,1)S(1)}, u32[]{:S(2)}, u32[]{:S(2)}) collective-permute-start(bf16[1024,128]{1,0:T(8,128)(2,1)S(1)} %collective-permute-done.3.refs_1_), channel_id=1, source_target_pairs={{0,128},{128,0},{1,129},{129,1},{2,130},{130,2},{3,131},{131,3},{4... | collective-permute-start | bytes 786440 | tf_op jit(solution)/shard_map/ppermute | solution.py:353
  100.8 1.3 collective-permute-start.8
  102.1 6.6 %collective-permute-start.10 = (f32[4,4,2,1,128]{4,2,1,0,3:T(2,128)S(1)}, f32[4,4,2,1,128]{4,2,1,0,3:T(2,128)S(1)}, u32[]{:S(2)}, u32[]{:S(2)}) collective-permute-start(f32[4,4,2,1,128]{4,2,1,0,3:T(2,128)S(1)} %bitcast.91), channel_id=1, source_target_pairs={{0,112},{1,113},{2,114},{3,115},{4,116},{5,117},{6,118},{7,119},{8... | collective-permute-start | bytes 49160 | tf_op jit(solution)/shard_map/ppermute | solution.py:370
  102.2 7.7 %collective-permute-start.11 = (f32[4,4,2,1,128]{4,2,1,0,3:T(2,128)S(1)}, f32[4,4,2,1,128]{4,2,1,0,3:T(2,128)S(1)}, u32[]{:S(2)}, u32[]{:S(2)}) collective-permute-start(f32[4,4,2,1,128]{4,2,1,0,3:T(2,128)S(1)} %bitcast.92), channel_id=1, source_target_pairs={{0,64},{1,65},{2,66},{3,67},{4,68},{5,69},{6,70},{7,71},{8,72},{9,... | collective-permute-start | bytes 49160 | tf_op jit(solution)/shard_map/ppermute | solution.py:370
  107.0 5.5 %collective-permute-start.9 = (f32[4,4,2,1,128]{4,2,1,0,3:T(2,128)S(1)}, f32[4,4,2,1,128]{4,2,1,0,3:T(2,128)S(1)}, u32[]{:S(2)}, u32[]{:S(2)}) collective-permute-start(f32[4,4,2,1,128]{4,2,1,0,3:T(2,128)S(1)} %bitcast.93), channel_id=1, source_target_pairs={{0,48},{1,49},{2,50},{3,51},{4,52},{5,53},{6,54},{7,55},{8,56},{9,... | collective-permute-start | bytes 49160 | tf_op jit(solution)/shard_map/ppermute | solution.py:370
  112.6 1.4 collective-permute-start.13
  113.9 3.8 %collective-permute-start.12 = (f32[4,4,2,1,128]{4,2,1,0,3:T(2,128)S(1)}, f32[4,4,2,1,128]{4,2,1,0,3:T(2,128)S(1)}, u32[]{:S(2)}, u32[]{:S(2)}) collective-permute-start(f32[4,4,2,1,128]{4,2,1,0,3:T(2,128)S(1)} %get-tuple-element.75), channel_id=1, source_target_pairs={{0,16},{1,17},{2,18},{3,19},{4,20},{5,21},{6,22},{7,23},{8,24},{9,... | collective-permute-start | bytes 49160 | tf_op jit(solution)/shard_map/ppermute | solution.py:370
  125.2 3.3 %collective-permute-start.17 = (bf16[1024,128]{1,0:T(8,128)(2,1)S(1)}, bf16[1024,128]{1,0:T(8,128)(2,1)S(1)}, u32[]{:S(2)}, u32[]{:S(2)}) collective-permute-start(bf16[1024,128]{1,0:T(8,128)(2,1)S(1)} %get-tuple-element.48), channel_id=1, source_target_pairs={{0,128},{128,0},{1,129},{129,1},{2,130},{130,2},{3,131},{131,3},{4... | collective-permute-start | bytes 786440 | tf_op jit(solution)/shard_map/ppermute | solution.py:353
  125.5 3.9 %collective-permute-start.16 = (bf16[1024,128]{1,0:T(8,128)(2,1)S(1)}, bf16[1024,128]{1,0:T(8,128)(2,1)S(1)}, u32[]{:S(2)}, u32[]{:S(2)}) collective-permute-start(bf16[1024,128]{1,0:T(8,128)(2,1)S(1)} %get-tuple-element.46), channel_id=1, source_target_pairs={{0,128},{128,0},{1,129},{129,1},{2,130},{130,2},{3,131},{131,3},{4... | collective-permute-start | bytes 786440 | tf_op jit(solution)/shard_map/ppermute | solution.py:353
  125.8 3.5 %collective-permute-start.19 = (bf16[1024,128]{1,0:T(8,128)(2,1)S(1)}, bf16[1024,128]{1,0:T(8,128)(2,1)}, u32[]{:S(2)}, u32[]{:S(2)}) collective-permute-start(bf16[1024,128]{1,0:T(8,128)(2,1)S(1)} %get-tuple-element.49), channel_id=1, source_target_pairs={{128,140},{129,141},{130,142},{131,143},{132,136},{133,137},{134,1... | collective-permute-start | bytes 786440 | tf_op jit(solution)/shard_map/ppermute | solution.py:370
  127.2 2.2 collective-permute-start.20
  129.3 6.7 %collective-permute-start.18 = (bf16[1024,128]{1,0:T(8,128)(2,1)}, bf16[1024,128]{1,0:T(8,128)(2,1)}, u32[]{:S(2)}, u32[]{:S(2)}) collective-permute-start(bf16[1024,128]{1,0:T(8,128)(2,1)} %add_convert_fusion), channel_id=1, source_target_pairs={{0,16},{1,17},{2,18},{3,19},{4,20},{5,21},{6,22},{7,23},{8,24},{9,... | collective-permute-start | bytes 786440 | tf_op jit(solution)/shard_map/ppermute | solution.py:370
  137.5 9.2 %collective-permute-start.23 = (bf16[256,128]{1,0:T(8,128)(2,1)S(1)}, bf16[256,128]{1,0:T(8,128)(2,1)S(1)}, u32[]{:S(2)}, u32[]{:S(2)}) collective-permute-start(bf16[256,128]{1,0:T(8,128)(2,1)S(1)} %get-tuple-element.83), channel_id=1, source_target_pairs={{0,64},{1,65},{2,66},{3,67},{4,68},{5,69},{6,70},{7,71},{8,72},{9,... | collective-permute-start | bytes 196616 | tf_op jit(solution)/shard_map/ppermute | solution.py:370
  139.7 7.0 %collective-permute-start.22 = (bf16[256,128]{1,0:T(8,128)(2,1)S(1)}, bf16[256,128]{1,0:T(8,128)(2,1)S(1)}, u32[]{:S(2)}, u32[]{:S(2)}) collective-permute-start(bf16[256,128]{1,0:T(8,128)(2,1)S(1)} %get-tuple-element.84), channel_id=1, source_target_pairs={{0,112},{1,113},{2,114},{3,115},{4,116},{5,117},{6,118},{7,119},{8... | collective-permute-start | bytes 196616 | tf_op jit(solution)/shard_map/ppermute | solution.py:370
  141.9 6.6 %collective-permute-start.21 = (bf16[256,128]{1,0:T(8,128)(2,1)S(1)}, bf16[256,128]{1,0:T(8,128)(2,1)S(1)}, u32[]{:S(2)}, u32[]{:S(2)}) collective-permute-start(bf16[256,128]{1,0:T(8,128)(2,1)S(1)} %get-tuple-element.85), channel_id=1, source_target_pairs={{0,48},{1,49},{2,50},{3,51},{4,52},{5,53},{6,54},{7,55},{8,56},{9,... | collective-permute-start | bytes 196616 | tf_op jit(solution)/shard_map/ppermute | solution.py:370
  152.7 10.7 %collective-permute-start.24 = (bf16[64,40,128]{2,1,0:T(8,128)(2,1)S(1)}, bf16[64,40,128]{2,1,0:T(8,128)(2,1)S(1)}, u32[]{:S(2)}, u32[]{:S(2)}) collective-permute-start(bf16[64,40,128]{2,1,0:T(8,128)(2,1)S(1)} %get-tuple-element.59), channel_id=1, source_target_pairs={{0,1},{1,0},{2,3},{3,2},{4,5},{5,4},{6,7},{7,6},{8,9},{9,8},{10,11... | collective-permute-start | bytes 1966088 | tf_op jit(solution)/shard_map/ppermute | solution.py:390
  154.2 10.6 %collective-permute-start.27 = (bf16[64,40,128]{2,1,0:T(8,128)(2,1)S(1)}, bf16[64,40,128]{2,1,0:T(8,128)(2,1)S(1)}, u32[]{:S(2)}, u32[]{:S(2)}) collective-permute-start(bf16[64,40,128]{2,1,0:T(8,128)(2,1)S(1)} %get-tuple-element.61), channel_id=1, source_target_pairs={{0,4},{1,5},{2,6},{3,7},{4,0},{5,1},{6,2},{7,3},{8,12},{9,13},{10,... | collective-permute-start | bytes 1966088 | tf_op jit(solution)/shard_map/ppermute | solution.py:390
  154.7 11.0 %collective-permute-start.30 = (bf16[64,40,128]{2,1,0:T(8,128)(2,1)S(1)}, bf16[64,40,128]{2,1,0:T(8,128)(2,1)S(1)}, u32[]{:S(2)}, u32[]{:S(2)}) collective-permute-start(bf16[64,40,128]{2,1,0:T(8,128)(2,1)S(1)} %get-tuple-element.63), channel_id=1, source_target_pairs={{0,16},{1,17},{2,18},{3,19},{4,20},{5,21},{6,22},{7,23},{8,24},{9,... | collective-permute-start | bytes 1966088 | tf_op jit(solution)/shard_map/ppermute | solution.py:390
  163.6 7.2 %collective-permute-start.25 = (bf16[32,40,128]{2,1,0:T(8,128)(2,1)S(1)}, bf16[32,40,128]{2,1,0:T(8,128)(2,1)S(1)}, u32[]{:S(2)}, u32[]{:S(2)}) collective-permute-start(bf16[32,40,128]{2,1,0:T(8,128)(2,1)S(1)} %slice.281), channel_id=1, source_target_pairs={{0,4},{1,5},{2,6},{3,7},{4,0},{5,1},{6,2},{7,3},{8,12},{9,13},{10,... | collective-permute-start | bytes 983048 | tf_op jit(solution)/shard_map/ppermute | solution.py:390
  165.0 7.2 %collective-permute-start.28 = (bf16[32,40,128]{2,1,0:T(8,128)(2,1)S(1)}, bf16[32,40,128]{2,1,0:T(8,128)(2,1)S(1)}, u32[]{:S(2)}, u32[]{:S(2)}) collective-permute-start(bf16[32,40,128]{2,1,0:T(8,128)(2,1)S(1)} %slice.280), channel_id=1, source_target_pairs={{0,16},{1,17},{2,18},{3,19},{4,20},{5,21},{6,22},{7,23},{8,24},{9,... | collective-permute-start | bytes 983048 | tf_op jit(solution)/shard_map/ppermute | solution.py:390
  165.9 7.2 %collective-permute-start.31 = (bf16[32,40,128]{2,1,0:T(8,128)(2,1)S(1)}, bf16[32,40,128]{2,1,0:T(8,128)(2,1)S(1)}, u32[]{:S(2)}, u32[]{:S(2)}) collective-permute-start(bf16[32,40,128]{2,1,0:T(8,128)(2,1)S(1)} %slice.279), channel_id=1, source_target_pairs={{0,1},{1,0},{2,3},{3,2},{4,5},{5,4},{6,7},{7,6},{8,9},{9,8},{10,11... | collective-permute-start | bytes 983048 | tf_op jit(solution)/shard_map/ppermute | solution.py:390
  170.8 5.4 %collective-permute-start.26 = (bf16[16,40,128]{2,1,0:T(8,128)(2,1)S(1)}, bf16[16,40,128]{2,1,0:T(8,128)(2,1)S(1)}, u32[]{:S(2)}, u32[]{:S(2)}) collective-permute-start(bf16[16,40,128]{2,1,0:T(8,128)(2,1)S(1)} %slice.284), channel_id=1, source_target_pairs={{0,16},{1,17},{2,18},{3,19},{4,20},{5,21},{6,22},{7,23},{8,24},{9,... | collective-permute-start | bytes 491528 | tf_op jit(solution)/shard_map/ppermute | solution.py:390
  172.2 5.4 %collective-permute-start.29 = (bf16[16,40,128]{2,1,0:T(8,128)(2,1)S(1)}, bf16[16,40,128]{2,1,0:T(8,128)(2,1)S(1)}, u32[]{:S(2)}, u32[]{:S(2)}) collective-permute-start(bf16[16,40,128]{2,1,0:T(8,128)(2,1)S(1)} %slice.283), channel_id=1, source_target_pairs={{0,1},{1,0},{2,3},{3,2},{4,5},{5,4},{6,7},{7,6},{8,9},{9,8},{10,11... | collective-permute-start | bytes 491528 | tf_op jit(solution)/shard_map/ppermute | solution.py:390
  173.3 5.4 %collective-permute-start.32 = (bf16[16,40,128]{2,1,0:T(8,128)(2,1)S(1)}, bf16[16,40,128]{2,1,0:T(8,128)(2,1)S(1)}, u32[]{:S(2)}, u32[]{:S(2)}) collective-permute-start(bf16[16,40,128]{2,1,0:T(8,128)(2,1)S(1)} %slice.282), channel_id=1, source_target_pairs={{0,4},{1,5},{2,6},{3,7},{4,0},{5,1},{6,2},{7,3},{8,12},{9,13},{10,... | collective-permute-start | bytes 491528 | tf_op jit(solution)/shard_map/ppermute | solution.py:390
  178.8 6.2 %collective-permute-start.33 = (bf16[3,4,40,128]{3,2,1,0:T(8,128)(2,1)S(1)}, bf16[3,4,40,128]{3,2,1,0:T(8,128)(2,1)S(1)}, u32[]{:S(2)}, u32[]{:S(2)}) collective-permute-start(bf16[3,4,40,128]{3,2,1,0:T(8,128)(2,1)S(1)} %get-tuple-element.80), channel_id=1, source_target_pairs={{0,12},{1,13},{2,14},{3,15},{4,8},{5,9},{6,10},{7,11},{8,4},{9,5},... | collective-permute-start | bytes 368648 | tf_op jit(solution)/shard_map/ppermute | solution.py:390
  180.3 7.0 %collective-permute-start.35 = (bf16[3,4,40,128]{3,2,1,0:T(8,128)(2,1)S(1)}, bf16[3,4,40,128]{3,2,1,0:T(8,128)(2,1)S(1)}, u32[]{:S(2)}, u32[]{:S(2)}) collective-permute-start(bf16[3,4,40,128]{3,2,1,0:T(8,128)(2,1)S(1)} %get-tuple-element.81), channel_id=1, source_target_pairs={{0,15},{1,14},{2,13},{3,12},{4,11},{5,10},{6,9},{7,8},{8,7},{9,6},... | collective-permute-start | bytes 368648 | tf_op jit(solution)/shard_map/ppermute | solution.py:390
  182.5 5.3 %collective-permute-start.34 = (bf16[3,4,40,128]{3,2,1,0:T(8,128)(2,1)S(1)}, bf16[3,4,40,128]{3,2,1,0:T(8,128)(2,1)S(1)}, u32[]{:S(2)}, u32[]{:S(2)}) collective-permute-start(bf16[3,4,40,128]{3,2,1,0:T(8,128)(2,1)S(1)} %get-tuple-element.82), channel_id=1, source_target_pairs={{0,3},{1,2},{2,1},{3,0},{4,7},{5,6},{6,5},{7,4},{8,11},{9,10},{10,... | collective-permute-start | bytes 368648 | tf_op jit(solution)/shard_map/ppermute | solution.py:390
  187.9 8.2 %collective-permute-start.36 = (bf16[3,4,40,128]{3,2,1,0:T(8,128)(2,1)S(1)}, bf16[3,4,40,128]{3,2,1,0:T(8,128)(2,1)S(1)}, u32[]{:S(2)}, u32[]{:S(2)}) collective-permute-start(bf16[3,4,40,128]{3,2,1,0:T(8,128)(2,1)S(1)} %fusion.3), channel_id=1, source_target_pairs={{0,112},{1,113},{2,114},{3,115},{4,116},{5,117},{6,118},{7,119},{8... | collective-permute-start | bytes 368648 | tf_op jit(solution)/shard_map/ppermute | solution.py:390
  196.1 6.8 %collective-permute-start.37 = (bf16[3,4,40,128]{3,2,1,0:T(8,128)(2,1)S(1)}, bf16[3,4,40,128]{3,2,1,0:T(8,128)(2,1)S(1)}, u32[]{:S(2)}, u32[]{:S(2)}) collective-permute-start(bf16[3,4,40,128]{3,2,1,0:T(8,128)(2,1)S(1)} %bitcast.86), channel_id=1, source_target_pairs={{0,48},{1,49},{2,50},{3,51},{4,52},{5,53},{6,54},{7,55},{8,56},{9,... | collective-permute-start | bytes 368648 | tf_op jit(solution)/shard_map/ppermute | solution.py:390
  202.9 7.3 %collective-permute-start.40 = (bf16[3,4,40,128]{3,2,1,0:T(8,128)(2,1)S(1)}, bf16[3,4,40,128]{3,2,1,0:T(8,128)(2,1)S(1)}, u32[]{:S(2)}, u32[]{:S(2)}) collective-permute-start(bf16[3,4,40,128]{3,2,1,0:T(8,128)(2,1)S(1)} %bitcast.81), channel_id=1, source_target_pairs={{0,15},{1,14},{2,13},{3,12},{4,11},{5,10},{6,9},{7,8},{8,7},{9,6},... | collective-permute-start | bytes 368648 | tf_op jit(solution)/shard_map/ppermute | solution.py:390
  204.8 5.6 %collective-permute-start.39 = (bf16[3,4,40,128]{3,2,1,0:T(8,128)(2,1)S(1)}, bf16[3,4,40,128]{3,2,1,0:T(8,128)(2,1)S(1)}, u32[]{:S(2)}, u32[]{:S(2)}) collective-permute-start(bf16[3,4,40,128]{3,2,1,0:T(8,128)(2,1)S(1)} %bitcast.82), channel_id=1, source_target_pairs={{0,3},{1,2},{2,1},{3,0},{4,7},{5,6},{6,5},{7,4},{8,11},{9,10},{10,... | collective-permute-start | bytes 368648 | tf_op jit(solution)/shard_map/ppermute | solution.py:390
  204.8 7.9 %collective-permute-start.38 = (bf16[3,4,40,128]{3,2,1,0:T(8,128)(2,1)S(1)}, bf16[3,4,40,128]{3,2,1,0:T(8,128)(2,1)S(1)}, u32[]{:S(2)}, u32[]{:S(2)}) collective-permute-start(bf16[3,4,40,128]{3,2,1,0:T(8,128)(2,1)S(1)} %bitcast.83), channel_id=1, source_target_pairs={{0,12},{1,13},{2,14},{3,15},{4,8},{5,9},{6,10},{7,11},{8,4},{9,5},... | collective-permute-start | bytes 368648 | tf_op jit(solution)/shard_map/ppermute | solution.py:390
  212.8 6.8 %collective-permute-start.41 = (bf16[16,40,128]{2,1,0:T(8,128)(2,1)S(1)}, bf16[16,40,128]{2,1,0:T(8,128)(2,1)S(1)}, u32[]{:S(2)}, u32[]{:S(2)}) collective-permute-start(bf16[16,40,128]{2,1,0:T(8,128)(2,1)S(1)} %get-tuple-element.79), channel_id=1, source_target_pairs={{0,1},{1,0},{2,3},{3,2},{4,5},{5,4},{6,7},{7,6},{8,9},{9,8},{10,11... | collective-permute-start | bytes 491528 | tf_op jit(solution)/shard_map/ppermute | solution.py:390
  216.3 5.3 %collective-permute-start.47 = (bf16[16,40,128]{2,1,0:T(8,128)(2,1)S(1)}, bf16[16,40,128]{2,1,0:T(8,128)(2,1)S(1)}, u32[]{:S(2)}, u32[]{:S(2)}) collective-permute-start(bf16[16,40,128]{2,1,0:T(8,128)(2,1)S(1)} %get-tuple-element.77), channel_id=1, source_target_pairs={{0,16},{1,17},{2,18},{3,19},{4,20},{5,21},{6,22},{7,23},{8,24},{9,... | collective-permute-start | bytes 491528 | tf_op jit(solution)/shard_map/ppermute | solution.py:390
  217.8 5.3 %collective-permute-start.44 = (bf16[16,40,128]{2,1,0:T(8,128)(2,1)S(1)}, bf16[16,40,128]{2,1,0:T(8,128)(2,1)S(1)}, u32[]{:S(2)}, u32[]{:S(2)}) collective-permute-start(bf16[16,40,128]{2,1,0:T(8,128)(2,1)S(1)} %get-tuple-element.78), channel_id=1, source_target_pairs={{0,4},{1,5},{2,6},{3,7},{4,0},{5,1},{6,2},{7,3},{8,12},{9,13},{10,... | collective-permute-start | bytes 491528 | tf_op jit(solution)/shard_map/ppermute | solution.py:390
  219.6 7.2 %collective-permute-start.42 = (bf16[32,40,128]{2,1,0:T(8,128)(2,1)S(1)}, bf16[32,40,128]{2,1,0:T(8,128)(2,1)S(1)}, u32[]{:S(2)}, u32[]{:S(2)}) collective-permute-start(bf16[32,40,128]{2,1,0:T(8,128)(2,1)S(1)} %pad_maximum_fusion.5), channel_id=1, source_target_pairs={{0,16},{1,17},{2,18},{3,19},{4,20},{5,21},{6,22},{7,23},{8,24},{9,... | collective-permute-start | bytes 983048 | tf_op jit(solution)/shard_map/ppermute | solution.py:390
  221.6 7.2 %collective-permute-start.48 = (bf16[32,40,128]{2,1,0:T(8,128)(2,1)S(1)}, bf16[32,40,128]{2,1,0:T(8,128)(2,1)S(1)}, u32[]{:S(2)}, u32[]{:S(2)}) collective-permute-start(bf16[32,40,128]{2,1,0:T(8,128)(2,1)S(1)} %pad_maximum_fusion.7), channel_id=1, source_target_pairs={{0,4},{1,5},{2,6},{3,7},{4,0},{5,1},{6,2},{7,3},{8,12},{9,13},{10,... | collective-permute-start | bytes 983048 | tf_op jit(solution)/shard_map/ppermute | solution.py:390
  223.2 7.4 %collective-permute-start.45 = (bf16[32,40,128]{2,1,0:T(8,128)(2,1)S(1)}, bf16[32,40,128]{2,1,0:T(8,128)(2,1)S(1)}, u32[]{:S(2)}, u32[]{:S(2)}) collective-permute-start(bf16[32,40,128]{2,1,0:T(8,128)(2,1)S(1)} %pad_maximum_fusion.6), channel_id=1, source_target_pairs={{0,1},{1,0},{2,3},{3,2},{4,5},{5,4},{6,7},{7,6},{8,9},{9,8},{10,11... | collective-permute-start | bytes 983048 | tf_op jit(solution)/shard_map/ppermute | solution.py:390
  226.9 14.6 %collective-permute-start.43 = (bf16[64,40,128]{2,1,0:T(8,128)(2,1)S(1)}, bf16[64,40,128]{2,1,0:T(8,128)(2,1)S(1)}, u32[]{:S(2)}, u32[]{:S(2)}) collective-permute-start(bf16[64,40,128]{2,1,0:T(8,128)(2,1)S(1)} %pad_maximum_fusion.1.rest_1_), channel_id=1, source_target_pairs={{0,4},{1,5},{2,6},{3,7},{4,0},{5,1},{6,2},{7,3},{8,12},{9,13},{10,... | collective-permute-start | bytes 1966088 | tf_op jit(solution)/shard_map/ppermute | solution.py:390
  228.9 10.7 %collective-permute-start.49 = (bf16[64,40,128]{2,1,0:T(8,128)(2,1)S(1)}, bf16[64,40,128]{2,1,0:T(8,128)(2,1)S(1)}, u32[]{:S(2)}, u32[]{:S(2)}) collective-permute-start(bf16[64,40,128]{2,1,0:T(8,128)(2,1)S(1)} %pad_maximum_fusion.3.rest_0_), channel_id=1, source_target_pairs={{0,1},{1,0},{2,3},{3,2},{4,5},{5,4},{6,7},{7,6},{8,9},{9,8},{10,11... | collective-permute-start | bytes 1966088 | tf_op jit(solution)/shard_map/ppermute | solution.py:390
  230.7 10.7 %collective-permute-start.46 = (bf16[64,40,128]{2,1,0:T(8,128)(2,1)S(1)}, bf16[64,40,128]{2,1,0:T(8,128)(2,1)S(1)}, u32[]{:S(2)}, u32[]{:S(2)}) collective-permute-start(bf16[64,40,128]{2,1,0:T(8,128)(2,1)S(1)} %pad_maximum_fusion.2.rest_2_), channel_id=1, source_target_pairs={{0,16},{1,17},{2,18},{3,19},{4,20},{5,21},{6,22},{7,23},{8,24},{9,... | collective-permute-start | bytes 1966088 | tf_op jit(solution)/shard_map/ppermute | solution.py:390
  (9 other events, 65.0 us)

commit v2 on v1

--- a/solution.py
+++ b/solution.py
@@ -546,8 +546,8 @@
     )(place, grad[0], *got, u, r, x, *slopes, weight_mid, weight_out)
     pairs = spread_weights(sum_weights(sums[:PARTS], sums[PARTS:]))
     grads = finish(tuple(range(PARTS)), 0, place, pairs[0::2], ())
-    grads = finish((0,), 1, place, pairs[1:2], grads)
-    grads = finish(tuple(range(1, PARTS)), 1, place, pairs[3::2], grads)
+    grads = finish((1,), 1, place, pairs[3:4], grads)
+    grads = finish((0, 2), 1, place, pairs[1::4], grads)
     return tuple(g[None] for g in grads)
 
 

time: 248 us -> 249 us (level)
  transfers between devices with their start and end apart: 50 -> 50, of which waited for: 31 -> 29; matrix products, arithmetic and copies ran while one was open for 1% -> 1% of each run, Pallas kernels for 3% -> 3%
where the time goes in v2:
time: 249 us; the launch traced here: 245 us
  waiting for transfers between devices  78 us (31%)
  starting transfers between devices  71.2 us (29%)
  blocking collectives  57.6 us (23%)
  Pallas kernels  31.2 us (13%)
  other arithmetic  3.73 us (1%)
    all_to_all x2, blocking collectives, exchange(): return lax.all_to_all(value, axes, split_axis=0, concat_axis=0, tiled=True)  57.6 us
    ppermute x26, waiting for transfers between devices, trade(): return lax.ppermute(value, AXES, pairs)  50.5 us
    ppermute x26, starting transfers between devices, trade(): return lax.ppermute(value, AXES, pairs)  32.8 us
    ppermute x18, starting transfers between devices, across(): return lax.ppermute(value, AXES, pairs)  25.7 us
    ppermute x18, waiting for transfers between devices, across(): return lax.ppermute(value, AXES, pairs)  24.4 us
    ppermute x6, starting transfers between devices, swap(): return lax.ppermute(value, 'side', [(0, 1), (1, 0)])  12.7 us
    pallas_call x3, Pallas kernels, finish(): pl.pallas_call(functools.partial(finish_kernel, parts, half), out_shape=[...  7.44 us
    pallas_call x1, Pallas kernels, on_device(): call(grad_kernel, [((QUART, EMB), F32)] * 2 + [((QUART, EMB), BF16)] * 4,...  6.14 us
  transfers between devices with their start and end apart: 50, of which 29 were waited for; matrix products, arithmetic and copies ran while one was open for 1% of the time, Pallas kernels for 3%

profile of v2, /device:TPU:2, one launch (start us, length us, event | category | flops | bytes accessed | tf_op | source)
XLA Modules:
  0.0 245.5 jit_solution(17244023643888495)
XLA Ops:
  0.6 1.6 shard_map.85
  2.3 26.7 %all_to_all.10 = s32[128,1,128]{2,1,0:T(1,128)S(1)} all-to-all(s32[128,1,128]{2,1,0:T(1,128)} %bitcast.95), channel_id=1, replica_groups=mesh['side'=2,'z'=8,'y'=4,'x'=4] {'z','y','x'}, dimensions={0} | all-to-all | bytes 131072 | tf_op jit(solution)/shard_map/all_to_all | solution.py:349
  30.1 2.0 shard_map.86
  32.1 30.9 %all_to_all.11 = bf16[128,8,384]{2,1,0:T(8,128)(2,1)} all-to-all(bf16[128,8,384]{2,1,0:T(8,128)(2,1)S(1)} %bitcast.66), channel_id=1, replica_groups=mesh['side'=2,'z'=8,'y'=4,'x'=4] {'z','y','x'}, dimensions={0} | all-to-all | bytes 1572864 | tf_op jit(solution)/shard_map/all_to_all | solution.py:349
  63.0 5.1 %shard_map.87 = (bf16[256,768]{1,0:T(8,128)(2,1)}, f32[256,128]{1,0:T(8,128)}, f32[256,128]{1,0:T(8,128)}, bf16[256,128]{1,0:T(8,128)(2,1)}) custom-call(s32[1,256]{1,0:T(1,128)} %get-tuple-element.38.position_ref, bf16[1024,384]{1,0:T(8,128)(2,1)} %bitcast.73, bf16[768,1024]{1,0:T(8,128)(2,1)} %bitcast.64, bf16[1024,1024]{1,0:T(8,128)(2,1)} %bitcast.61, ...), custom_call_target="tpu_custom_call" | custom-call | tf_op jit(solution)/shard_map/pallas_call | solution.py:494
  68.2 3.4 %collective-permute-start.1 = (bf16[256,128]{1,0:T(8,128)(2,1)}, bf16[256,128]{1,0:T(8,128)(2,1)S(1)}, u32[]{:S(2)}, u32[]{:S(2)}) collective-permute-start(bf16[256,128]{1,0:T(8,128)(2,1)} %get-tuple-element.40), channel_id=1, source_target_pairs={{0,112},{1,113},{2,114},{3,115},{4,116},{5,117},{6,118},{7,119},{8... | collective-permute-start | bytes 196616 | tf_op jit(solution)/shard_map/ppermute | solution.py:370
  71.6 3.1 %collective-permute-start = (bf16[256,128]{1,0:T(8,128)(2,1)}, bf16[256,128]{1,0:T(8,128)(2,1)S(1)}, u32[]{:S(2)}, u32[]{:S(2)}) collective-permute-start(bf16[256,128]{1,0:T(8,128)(2,1)} %get-tuple-element.40), channel_id=1, source_target_pairs={{0,48},{1,49},{2,50},{3,51},{4,52},{5,53},{6,54},{7,55},{8,56},{9,... | collective-permute-start | bytes 196616 | tf_op jit(solution)/shard_map/ppermute | solution.py:370
  75.6 3.4 %collective-permute-done = bf16[256,128]{1,0:T(8,128)(2,1)S(1)} collective-permute-done((bf16[256,128]{1,0:T(8,128)(2,1)}, bf16[256,128]{1,0:T(8,128)(2,1)S(1)}, u32[]{:S(2)}, u32[]{:S(2)}) %collective-permute-start) | collective-permute-done | bytes 65568 | tf_op jit(solution)/shard_map/ppermute | solution.py:370
  80.5 5.0 %collective-permute-done.3.refs_1_ = bf16[1024,128]{1,0:T(8,128)(2,1)S(1)} collective-permute-done((bf16[1024,128]{1,0:T(8,128)(2,1)S(1)}, bf16[1024,128]{1,0:T(8,128)(2,1)S(1)}, u32[]{:S(2)}, u32[]{:S(2)}) %collective-permute-start.3) | collective-permute-done | bytes 262176 | tf_op jit(solution)/shard_map/ppermute | solution.py:370
  85.5 11.5 %collective-permute-start.7 = (bf16[1024,128]{1,0:T(8,128)(2,1)S(1)}, bf16[1024,128]{1,0:T(8,128)(2,1)S(1)}, u32[]{:S(2)}, u32[]{:S(2)}) collective-permute-start(bf16[1024,128]{1,0:T(8,128)(2,1)S(1)} %collective-permute-done.3.refs_1_), channel_id=1, source_target_pairs={{0,128},{128,0},{1,129},{129,1},{2,130},{130,2},{3,131},{131,3},{4... | collective-permute-start | bytes 786440 | tf_op jit(solution)/shard_map/ppermute | solution.py:353
  98.2 2.6 %shard_map.88 = (f32[16,1,128]{2,1,0:T(1,128)S(1)}, f32[16,1,128]{2,1,0:T(1,128)S(1)}) custom-call(s32[1]{0:T(128)} %bitcast.3.side_ref, bf16[1024,128]{1,0:T(8,128)(2,1)S(1)} %constant_dynamic-update-slice_fusion.refs_0_, bf16[1024,128]{1,0:T(8,128)(2,1)S(1)} %collective-permute-done.3.refs_1_, bf16[1024,128]{1,0:T(8,128)(2,1)S(1)} %collective-permute-done.4.refs_2_, ...), custom_call_target="tpu_custom_call" | custom-call | tf_op jit(solution)/shard_map/pallas_call | solution.py:509
  102.2 4.8 %collective-permute-start.11 = (f32[4,4,2,1,128]{4,2,1,0,3:T(2,128)S(1)}, f32[4,4,2,1,128]{4,2,1,0,3:T(2,128)S(1)}, u32[]{:S(2)}, u32[]{:S(2)}) collective-permute-start(f32[4,4,2,1,128]{4,2,1,0,3:T(2,128)S(1)} %bitcast.92), channel_id=1, source_target_pairs={{0,64},{1,65},{2,66},{3,67},{4,68},{5,69},{6,70},{7,71},{8,72},{9,... | collective-permute-start | bytes 49160 | tf_op jit(solution)/shard_map/ppermute | solution.py:370
  107.0 1.7 collective-permute-start.9
  109.9 2.6 %collective-permute-done.9 = f32[4,4,2,1,128]{4,2,1,0,3:T(2,128)S(1)} collective-permute-done((f32[4,4,2,1,128]{4,2,1,0,3:T(2,128)S(1)}, f32[4,4,2,1,128]{4,2,1,0,3:T(2,128)S(1)}, u32[]{:S(2)}, u32[]{:S(2)}) %collective-permute-start.9) | collective-permute-done | bytes 16416 | tf_op jit(solution)/shard_map/ppermute | solution.py:370
  114.1 3.7 %collective-permute-done.12 = f32[4,4,2,1,128]{4,2,1,0,3:T(2,128)S(1)} collective-permute-done((f32[4,4,2,1,128]{4,2,1,0,3:T(2,128)S(1)}, f32[4,4,2,1,128]{4,2,1,0,3:T(2,128)S(1)}, u32[]{:S(2)}, u32[]{:S(2)}) %collective-permute-start.12) | collective-permute-done | bytes 16416 | tf_op jit(solution)/shard_map/ppermute | solution.py:370
  119.1 6.1 %shard_map.89 = (f32[1024,128]{1,0:T(8,128)S(1)}, f32[1024,128]{1,0:T(8,128)S(1)}, bf16[1024,128]{1,0:T(8,128)(2,1)S(1)}, bf16[1024,128]{1,0:T(8,128)(2,1)S(1)},...) custom-call(s32[1]{0:T(128)} %bitcast.3.side_ref, ...), custom_call_target="tpu_custom_call" | custom-call | tf_op jit(solution)/shard_map/pallas_call | solution.py:514
  129.4 6.7 %collective-permute-done.18 = bf16[1024,128]{1,0:T(8,128)(2,1)} collective-permute-done((bf16[1024,128]{1,0:T(8,128)(2,1)}, bf16[1024,128]{1,0:T(8,128)(2,1)}, u32[]{:S(2)}, u32[]{:S(2)}) %collective-permute-start.18) | collective-permute-done | bytes 262176 | tf_op jit(solution)/shard_map/ppermute | solution.py:370
  136.0 1.4 fusion.7
  137.5 2.2 collective-permute-start.23
  139.7 2.2 collective-permute-start.22
  141.9 2.5 %collective-permute-start.21 = (bf16[256,128]{1,0:T(8,128)(2,1)S(1)}, bf16[256,128]{1,0:T(8,128)(2,1)S(1)}, u32[]{:S(2)}, u32[]{:S(2)}) collective-permute-start(bf16[256,128]{1,0:T(8,128)(2,1)S(1)} %get-tuple-element.85), channel_id=1, source_target_pairs={{0,48},{1,49},{2,50},{3,51},{4,52},{5,53},{6,54},{7,55},{8,56},{9,... | collective-permute-start | bytes 196616 | tf_op jit(solution)/shard_map/ppermute | solution.py:370
  144.6 2.1 shard_map.90
  146.7 1.8 collective-permute-done.21.sent0_ref
  148.5 4.2 %shard_map.91 = (bf16[64,40,128]{2,1,0:T(8,128)(2,1)S(1)}, bf16[64,40,128]{2,1,0:T(8,128)(2,1)S(1)}, bf16[64,40,128]{2,1,0:T(8,128)(2,1)S(1)}, bf16[64,40,128]{2...) custom-call(s32[3]{0:T(128)S(1)} %pad_add_fusion.place_ref, ...), custom_call_target="tpu_custom_call" | custom-call | tf_op jit(solution)/shard_map/pallas_call | solution.py:540
  152.7 1.5 collective-permute-start.24
  155.3 8.1 %collective-permute-done.24 = bf16[64,40,128]{2,1,0:T(8,128)(2,1)S(1)} collective-permute-done((bf16[64,40,128]{2,1,0:T(8,128)(2,1)S(1)}, bf16[64,40,128]{2,1,0:T(8,128)(2,1)S(1)}, u32[]{:S(2)}, u32[]{:S(2)}) %collective-permute-start.24) | collective-permute-done | bytes 655392 | tf_op jit(solution)/shard_map/ppermute | solution.py:390
  166.7 4.0 %collective-permute-done.25 = bf16[32,40,128]{2,1,0:T(8,128)(2,1)S(1)} collective-permute-done((bf16[32,40,128]{2,1,0:T(8,128)(2,1)S(1)}, bf16[32,40,128]{2,1,0:T(8,128)(2,1)S(1)}, u32[]{:S(2)}, u32[]{:S(2)}) %collective-permute-start.25) | collective-permute-done | bytes 327712 | tf_op jit(solution)/shard_map/ppermute | solution.py:390
  173.3 1.5 collective-permute-start.32
  178.8 1.5 collective-permute-start.33
  180.3 2.2 collective-permute-start.35
  185.0 2.3 collective-permute-done.35
  187.9 2.0 collective-permute-start.36
  189.8 6.2 %collective-permute-done.36 = bf16[3,4,40,128]{3,2,1,0:T(8,128)(2,1)S(1)} collective-permute-done((bf16[3,4,40,128]{3,2,1,0:T(8,128)(2,1)S(1)}, bf16[3,4,40,128]{3,2,1,0:T(8,128)(2,1)S(1)}, u32[]{:S(2)}, u32[]{:S(2)}) %collective-permute-start.36) | collective-permute-done | bytes 122912 | tf_op jit(solution)/shard_map/ppermute | solution.py:390
  196.8 6.1 %collective-permute-done.37 = bf16[3,4,40,128]{3,2,1,0:T(8,128)(2,1)S(1)} collective-permute-done((bf16[3,4,40,128]{3,2,1,0:T(8,128)(2,1)S(1)}, bf16[3,4,40,128]{3,2,1,0:T(8,128)(2,1)S(1)}, u32[]{:S(2)}, u32[]{:S(2)}) %collective-permute-start.37) | collective-permute-done | bytes 122912 | tf_op jit(solution)/shard_map/ppermute | solution.py:390
  202.9 1.8 collective-permute-start.40
  204.8 2.9 %collective-permute-start.38 = (bf16[3,4,40,128]{3,2,1,0:T(8,128)(2,1)S(1)}, bf16[3,4,40,128]{3,2,1,0:T(8,128)(2,1)S(1)}, u32[]{:S(2)}, u32[]{:S(2)}) collective-permute-start(bf16[3,4,40,128]{3,2,1,0:T(8,128)(2,1)S(1)} %bitcast.83), channel_id=1, source_target_pairs={{0,12},{1,13},{2,14},{3,15},{4,8},{5,9},{6,10},{7,11},{8,4},{9,5},... | collective-permute-start | bytes 368648 | tf_op jit(solution)/shard_map/ppermute | solution.py:390
  207.7 3.0 %collective-permute-done.40 = bf16[3,4,40,128]{3,2,1,0:T(8,128)(2,1)S(1)} collective-permute-done((bf16[3,4,40,128]{3,2,1,0:T(8,128)(2,1)S(1)}, bf16[3,4,40,128]{3,2,1,0:T(8,128)(2,1)S(1)}, u32[]{:S(2)}, u32[]{:S(2)}) %collective-permute-start.40) | collective-permute-done | bytes 122912 | tf_op jit(solution)/shard_map/ppermute | solution.py:390
  210.8 1.9 collective-permute-done.38
  212.8 2.8 %collective-permute-start.41 = (bf16[16,40,128]{2,1,0:T(8,128)(2,1)S(1)}, bf16[16,40,128]{2,1,0:T(8,128)(2,1)S(1)}, u32[]{:S(2)}, u32[]{:S(2)}) collective-permute-start(bf16[16,40,128]{2,1,0:T(8,128)(2,1)S(1)} %get-tuple-element.79), channel_id=1, source_target_pairs={{0,16},{1,17},{2,18},{3,19},{4,20},{5,21},{6,22},{7,23},{8,24},{9,... | collective-permute-start | bytes 491528 | tf_op jit(solution)/shard_map/ppermute | solution.py:390
  215.6 3.6 %collective-permute-start.47 = (bf16[16,40,128]{2,1,0:T(8,128)(2,1)S(1)}, bf16[16,40,128]{2,1,0:T(8,128)(2,1)S(1)}, u32[]{:S(2)}, u32[]{:S(2)}) collective-permute-start(bf16[16,40,128]{2,1,0:T(8,128)(2,1)S(1)} %get-tuple-element.77), channel_id=1, source_target_pairs={{0,1},{1,0},{2,3},{3,2},{4,5},{5,4},{6,7},{7,6},{8,9},{9,8},{10,11... | collective-permute-start | bytes 491528 | tf_op jit(solution)/shard_map/ppermute | solution.py:390
  219.2 2.1 collective-permute-start.42
  222.9 1.6 collective-permute-done.44
  225.1 2.9 %collective-permute-done.42 = bf16[32,40,128]{2,1,0:T(8,128)(2,1)S(1)} collective-permute-done((bf16[32,40,128]{2,1,0:T(8,128)(2,1)S(1)}, bf16[32,40,128]{2,1,0:T(8,128)(2,1)S(1)}, u32[]{:S(2)}, u32[]{:S(2)}) %collective-permute-start.42) | collective-permute-done | bytes 327712 | tf_op jit(solution)/shard_map/ppermute | solution.py:390
  228.1 2.1 collective-permute-start.43
  232.2 3.1 %shard_map.92 = (f32[768,1024]{1,0:T(8,128)}, f32[1024,1024]{1,0:T(8,128)}, f32[1024,128]{1,0:T(8,128)}) custom-call(s32[3]{0:T(128)S(1)} %pad_add_fusion.place_ref, bf16[64,40,128]{2,1,0:T(8,128)(2,1)S(1)} %pad_maximum_fusion.1.rest_0_, bf16[64,40,128]{2,1,0:T(8,128)(2,1)S(1)} %pad_maximum_fusion.3.rest_1_, bf16[64,40,128]{2,1,0:T(8,128)(2,1)S(1)} %pad_maximum_fusion.2.rest_2_), custom_call_target="tpu_custom_call" | custom-call | bytes 5898240 | tf_op jit(solution)/shard_map/pallas_call | solution.py:121
  235.3 5.6 %collective-permute-done.49.rest_0_ = bf16[64,40,128]{2,1,0:T(8,128)(2,1)S(1)} collective-permute-done((bf16[64,40,128]{2,1,0:T(8,128)(2,1)S(1)}, bf16[64,40,128]{2,1,0:T(8,128)(2,1)S(1)}, u32[]{:S(2)}, u32[]{:S(2)}) %collective-permute-start.49) | collective-permute-done | bytes 655392 | tf_op jit(solution)/shard_map/ppermute | solution.py:390
  240.9 1.9 shard_map.93
  242.8 2.5 %shard_map.94 = (f32[768,1024]{1,0:T(8,128)}, f32[1024,1024]{1,0:T(8,128)}, f32[1024,128]{1,0:T(8,128)}) custom-call(s32[3]{0:T(128)S(1)} %pad_add_fusion.place_ref, bf16[64,40,128]{2,1,0:T(8,128)(2,1)S(1)} %collective-permute-done.43.rest_0_, ...), custom_call_target="tpu_custom_call", output_to_operand_aliasing={{0}: (3, {}), {1}: (4, {}), {2}: (5, {})} | custom-call | bytes 3932160 | tf_op jit(solution)/shard_map/pallas_call | solution.py:121
  (128 shorter events, 33.7 us)
Async XLA Ops:
  68.1 10.9 %collective-permute-start.2 = (bf16[256,128]{1,0:T(8,128)(2,1)}, bf16[256,128]{1,0:T(8,128)(2,1)S(1)}, u32[]{:S(2)}, u32[]{:S(2)}) collective-permute-start(bf16[256,128]{1,0:T(8,128)(2,1)} %get-tuple-element.40), channel_id=1, source_target_pairs={{0,64},{1,65},{2,66},{3,67},{4,68},{5,69},{6,70},{7,71},{8,72},{9,... | collective-permute-start | bytes 196616 | tf_op jit(solution)/shard_map/ppermute | solution.py:370
  68.2 10.7 %collective-permute-start.1 = (bf16[256,128]{1,0:T(8,128)(2,1)}, bf16[256,128]{1,0:T(8,128)(2,1)S(1)}, u32[]{:S(2)}, u32[]{:S(2)}) collective-permute-start(bf16[256,128]{1,0:T(8,128)(2,1)} %get-tuple-element.40), channel_id=1, source_target_pairs={{0,112},{1,113},{2,114},{3,115},{4,116},{5,117},{6,118},{7,119},{8... | collective-permute-start | bytes 196616 | tf_op jit(solution)/shard_map/ppermute | solution.py:370
  71.6 7.4 %collective-permute-start = (bf16[256,128]{1,0:T(8,128)(2,1)}, bf16[256,128]{1,0:T(8,128)(2,1)S(1)}, u32[]{:S(2)}, u32[]{:S(2)}) collective-permute-start(bf16[256,128]{1,0:T(8,128)(2,1)} %get-tuple-element.40), channel_id=1, source_target_pairs={{0,48},{1,49},{2,50},{3,51},{4,52},{5,53},{6,54},{7,55},{8,56},{9,... | collective-permute-start | bytes 196616 | tf_op jit(solution)/shard_map/ppermute | solution.py:370
  79.0 6.5 %collective-permute-start.3 = (bf16[1024,128]{1,0:T(8,128)(2,1)S(1)}, bf16[1024,128]{1,0:T(8,128)(2,1)S(1)}, u32[]{:S(2)}, u32[]{:S(2)}) collective-permute-start(bf16[1024,128]{1,0:T(8,128)(2,1)S(1)} %constant_dynamic-update-slice_fusion.refs_0_), channel_id=1, source_target_pairs={{0,16},{1,17},{2,18},{3,19},{4,20},{5,21},{6,22},{7,23},{8,24},{9,... | collective-permute-start | bytes 786440 | tf_op jit(solution)/shard_map/ppermute | solution.py:370
  79.1 17.9 %collective-permute-start.5 = (bf16[1024,128]{1,0:T(8,128)(2,1)S(1)}, bf16[1024,128]{1,0:T(8,128)(2,1)S(1)}, u32[]{:S(2)}, u32[]{:S(2)}) collective-permute-start(bf16[1024,128]{1,0:T(8,128)(2,1)S(1)} %constant_dynamic-update-slice_fusion.refs_0_), channel_id=1, source_target_pairs={{128,136},{129,137},{130,138},{131,139},{132,140},{133,141},{134,1... | collective-permute-start | bytes 786440 | tf_op jit(solution)/shard_map/ppermute | solution.py:370
  79.8 17.2 %collective-permute-start.4 = (bf16[1024,128]{1,0:T(8,128)(2,1)S(1)}, bf16[1024,128]{1,0:T(8,128)(2,1)S(1)}, u32[]{:S(2)}, u32[]{:S(2)}) collective-permute-start(bf16[1024,128]{1,0:T(8,128)(2,1)S(1)} %constant_dynamic-update-slice_fusion.refs_0_), channel_id=1, source_target_pairs={{128,140},{129,141},{130,142},{131,143},{132,136},{133,137},{134,1... | collective-permute-start | bytes 786440 | tf_op jit(solution)/shard_map/ppermute | solution.py:370
  85.5 11.5 %collective-permute-start.6 = (bf16[1024,128]{1,0:T(8,128)(2,1)S(1)}, bf16[1024,128]{1,0:T(8,128)(2,1)S(1)}, u32[]{:S(2)}, u32[]{:S(2)}) collective-permute-start(bf16[1024,128]{1,0:T(8,128)(2,1)S(1)} %constant_dynamic-update-slice_fusion.refs_0_), channel_id=1, source_target_pairs={{0,128},{128,0},{1,129},{129,1},{2,130},{130,2},{3,131},{131,3},{4... | collective-permute-start | bytes 786440 | tf_op jit(solution)/shard_map/ppermute | solution.py:353
  85.5 12.7 %collective-permute-start.7 = (bf16[1024,128]{1,0:T(8,128)(2,1)S(1)}, bf16[1024,128]{1,0:T(8,128)(2,1)S(1)}, u32[]{:S(2)}, u32[]{:S(2)}) collective-permute-start(bf16[1024,128]{1,0:T(8,128)(2,1)S(1)} %collective-permute-done.3.refs_1_), channel_id=1, source_target_pairs={{0,128},{128,0},{1,129},{129,1},{2,130},{130,2},{3,131},{131,3},{4... | collective-permute-start | bytes 786440 | tf_op jit(solution)/shard_map/ppermute | solution.py:353
  100.8 1.3 collective-permute-start.8
  102.1 6.6 %collective-permute-start.10 = (f32[4,4,2,1,128]{4,2,1,0,3:T(2,128)S(1)}, f32[4,4,2,1,128]{4,2,1,0,3:T(2,128)S(1)}, u32[]{:S(2)}, u32[]{:S(2)}) collective-permute-start(f32[4,4,2,1,128]{4,2,1,0,3:T(2,128)S(1)} %bitcast.91), channel_id=1, source_target_pairs={{0,112},{1,113},{2,114},{3,115},{4,116},{5,117},{6,118},{7,119},{8... | collective-permute-start | bytes 49160 | tf_op jit(solution)/shard_map/ppermute | solution.py:370
  102.2 7.7 %collective-permute-start.11 = (f32[4,4,2,1,128]{4,2,1,0,3:T(2,128)S(1)}, f32[4,4,2,1,128]{4,2,1,0,3:T(2,128)S(1)}, u32[]{:S(2)}, u32[]{:S(2)}) collective-permute-start(f32[4,4,2,1,128]{4,2,1,0,3:T(2,128)S(1)} %bitcast.92), channel_id=1, source_target_pairs={{0,64},{1,65},{2,66},{3,67},{4,68},{5,69},{6,70},{7,71},{8,72},{9,... | collective-permute-start | bytes 49160 | tf_op jit(solution)/shard_map/ppermute | solution.py:370
  107.0 5.5 %collective-permute-start.9 = (f32[4,4,2,1,128]{4,2,1,0,3:T(2,128)S(1)}, f32[4,4,2,1,128]{4,2,1,0,3:T(2,128)S(1)}, u32[]{:S(2)}, u32[]{:S(2)}) collective-permute-start(f32[4,4,2,1,128]{4,2,1,0,3:T(2,128)S(1)} %bitcast.93), channel_id=1, source_target_pairs={{0,48},{1,49},{2,50},{3,51},{4,52},{5,53},{6,54},{7,55},{8,56},{9,... | collective-permute-start | bytes 49160 | tf_op jit(solution)/shard_map/ppermute | solution.py:370
  112.6 1.4 collective-permute-start.13
  113.9 3.8 %collective-permute-start.12 = (f32[4,4,2,1,128]{4,2,1,0,3:T(2,128)S(1)}, f32[4,4,2,1,128]{4,2,1,0,3:T(2,128)S(1)}, u32[]{:S(2)}, u32[]{:S(2)}) collective-permute-start(f32[4,4,2,1,128]{4,2,1,0,3:T(2,128)S(1)} %get-tuple-element.75), channel_id=1, source_target_pairs={{0,16},{1,17},{2,18},{3,19},{4,20},{5,21},{6,22},{7,23},{8,24},{9,... | collective-permute-start | bytes 49160 | tf_op jit(solution)/shard_map/ppermute | solution.py:370
  125.2 3.3 %collective-permute-start.17 = (bf16[1024,128]{1,0:T(8,128)(2,1)S(1)}, bf16[1024,128]{1,0:T(8,128)(2,1)S(1)}, u32[]{:S(2)}, u32[]{:S(2)}) collective-permute-start(bf16[1024,128]{1,0:T(8,128)(2,1)S(1)} %get-tuple-element.48), channel_id=1, source_target_pairs={{0,128},{128,0},{1,129},{129,1},{2,130},{130,2},{3,131},{131,3},{4... | collective-permute-start | bytes 786440 | tf_op jit(solution)/shard_map/ppermute | solution.py:353
  125.5 3.9 %collective-permute-start.16 = (bf16[1024,128]{1,0:T(8,128)(2,1)S(1)}, bf16[1024,128]{1,0:T(8,128)(2,1)S(1)}, u32[]{:S(2)}, u32[]{:S(2)}) collective-permute-start(bf16[1024,128]{1,0:T(8,128)(2,1)S(1)} %get-tuple-element.46), channel_id=1, source_target_pairs={{0,128},{128,0},{1,129},{129,1},{2,130},{130,2},{3,131},{131,3},{4... | collective-permute-start | bytes 786440 | tf_op jit(solution)/shard_map/ppermute | solution.py:353
  125.8 3.5 %collective-permute-start.19 = (bf16[1024,128]{1,0:T(8,128)(2,1)S(1)}, bf16[1024,128]{1,0:T(8,128)(2,1)}, u32[]{:S(2)}, u32[]{:S(2)}) collective-permute-start(bf16[1024,128]{1,0:T(8,128)(2,1)S(1)} %get-tuple-element.49), channel_id=1, source_target_pairs={{128,140},{129,141},{130,142},{131,143},{132,136},{133,137},{134,1... | collective-permute-start | bytes 786440 | tf_op jit(solution)/shard_map/ppermute | solution.py:370
  127.2 2.2 collective-permute-start.20
  129.3 6.7 %collective-permute-start.18 = (bf16[1024,128]{1,0:T(8,128)(2,1)}, bf16[1024,128]{1,0:T(8,128)(2,1)}, u32[]{:S(2)}, u32[]{:S(2)}) collective-permute-start(bf16[1024,128]{1,0:T(8,128)(2,1)} %add_convert_fusion), channel_id=1, source_target_pairs={{0,16},{1,17},{2,18},{3,19},{4,20},{5,21},{6,22},{7,23},{8,24},{9,... | collective-permute-start | bytes 786440 | tf_op jit(solution)/shard_map/ppermute | solution.py:370
  137.5 9.2 %collective-permute-start.23 = (bf16[256,128]{1,0:T(8,128)(2,1)S(1)}, bf16[256,128]{1,0:T(8,128)(2,1)S(1)}, u32[]{:S(2)}, u32[]{:S(2)}) collective-permute-start(bf16[256,128]{1,0:T(8,128)(2,1)S(1)} %get-tuple-element.83), channel_id=1, source_target_pairs={{0,64},{1,65},{2,66},{3,67},{4,68},{5,69},{6,70},{7,71},{8,72},{9,... | collective-permute-start | bytes 196616 | tf_op jit(solution)/shard_map/ppermute | solution.py:370
  139.7 7.0 %collective-permute-start.22 = (bf16[256,128]{1,0:T(8,128)(2,1)S(1)}, bf16[256,128]{1,0:T(8,128)(2,1)S(1)}, u32[]{:S(2)}, u32[]{:S(2)}) collective-permute-start(bf16[256,128]{1,0:T(8,128)(2,1)S(1)} %get-tuple-element.84), channel_id=1, source_target_pairs={{0,112},{1,113},{2,114},{3,115},{4,116},{5,117},{6,118},{7,119},{8... | collective-permute-start | bytes 196616 | tf_op jit(solution)/shard_map/ppermute | solution.py:370
  141.9 6.6 %collective-permute-start.21 = (bf16[256,128]{1,0:T(8,128)(2,1)S(1)}, bf16[256,128]{1,0:T(8,128)(2,1)S(1)}, u32[]{:S(2)}, u32[]{:S(2)}) collective-permute-start(bf16[256,128]{1,0:T(8,128)(2,1)S(1)} %get-tuple-element.85), channel_id=1, source_target_pairs={{0,48},{1,49},{2,50},{3,51},{4,52},{5,53},{6,54},{7,55},{8,56},{9,... | collective-permute-start | bytes 196616 | tf_op jit(solution)/shard_map/ppermute | solution.py:370
  152.7 10.7 %collective-permute-start.24 = (bf16[64,40,128]{2,1,0:T(8,128)(2,1)S(1)}, bf16[64,40,128]{2,1,0:T(8,128)(2,1)S(1)}, u32[]{:S(2)}, u32[]{:S(2)}) collective-permute-start(bf16[64,40,128]{2,1,0:T(8,128)(2,1)S(1)} %get-tuple-element.59), channel_id=1, source_target_pairs={{0,1},{1,0},{2,3},{3,2},{4,5},{5,4},{6,7},{7,6},{8,9},{9,8},{10,11... | collective-permute-start | bytes 1966088 | tf_op jit(solution)/shard_map/ppermute | solution.py:390
  154.2 10.6 %collective-permute-start.27 = (bf16[64,40,128]{2,1,0:T(8,128)(2,1)S(1)}, bf16[64,40,128]{2,1,0:T(8,128)(2,1)S(1)}, u32[]{:S(2)}, u32[]{:S(2)}) collective-permute-start(bf16[64,40,128]{2,1,0:T(8,128)(2,1)S(1)} %get-tuple-element.61), channel_id=1, source_target_pairs={{0,4},{1,5},{2,6},{3,7},{4,0},{5,1},{6,2},{7,3},{8,12},{9,13},{10,... | collective-permute-start | bytes 1966088 | tf_op jit(solution)/shard_map/ppermute | solution.py:390
  154.7 11.0 %collective-permute-start.30 = (bf16[64,40,128]{2,1,0:T(8,128)(2,1)S(1)}, bf16[64,40,128]{2,1,0:T(8,128)(2,1)S(1)}, u32[]{:S(2)}, u32[]{:S(2)}) collective-permute-start(bf16[64,40,128]{2,1,0:T(8,128)(2,1)S(1)} %get-tuple-element.63), channel_id=1, source_target_pairs={{0,16},{1,17},{2,18},{3,19},{4,20},{5,21},{6,22},{7,23},{8,24},{9,... | collective-permute-start | bytes 1966088 | tf_op jit(solution)/shard_map/ppermute | solution.py:390
  163.6 7.2 %collective-permute-start.25 = (bf16[32,40,128]{2,1,0:T(8,128)(2,1)S(1)}, bf16[32,40,128]{2,1,0:T(8,128)(2,1)S(1)}, u32[]{:S(2)}, u32[]{:S(2)}) collective-permute-start(bf16[32,40,128]{2,1,0:T(8,128)(2,1)S(1)} %slice.281), channel_id=1, source_target_pairs={{0,4},{1,5},{2,6},{3,7},{4,0},{5,1},{6,2},{7,3},{8,12},{9,13},{10,... | collective-permute-start | bytes 983048 | tf_op jit(solution)/shard_map/ppermute | solution.py:390
  165.0 7.2 %collective-permute-start.28 = (bf16[32,40,128]{2,1,0:T(8,128)(2,1)S(1)}, bf16[32,40,128]{2,1,0:T(8,128)(2,1)S(1)}, u32[]{:S(2)}, u32[]{:S(2)}) collective-permute-start(bf16[32,40,128]{2,1,0:T(8,128)(2,1)S(1)} %slice.280), channel_id=1, source_target_pairs={{0,16},{1,17},{2,18},{3,19},{4,20},{5,21},{6,22},{7,23},{8,24},{9,... | collective-permute-start | bytes 983048 | tf_op jit(solution)/shard_map/ppermute | solution.py:390
  165.9 7.2 %collective-permute-start.31 = (bf16[32,40,128]{2,1,0:T(8,128)(2,1)S(1)}, bf16[32,40,128]{2,1,0:T(8,128)(2,1)S(1)}, u32[]{:S(2)}, u32[]{:S(2)}) collective-permute-start(bf16[32,40,128]{2,1,0:T(8,128)(2,1)S(1)} %slice.279), channel_id=1, source_target_pairs={{0,1},{1,0},{2,3},{3,2},{4,5},{5,4},{6,7},{7,6},{8,9},{9,8},{10,11... | collective-permute-start | bytes 983048 | tf_op jit(solution)/shard_map/ppermute | solution.py:390
  170.8 5.4 %collective-permute-start.26 = (bf16[16,40,128]{2,1,0:T(8,128)(2,1)S(1)}, bf16[16,40,128]{2,1,0:T(8,128)(2,1)S(1)}, u32[]{:S(2)}, u32[]{:S(2)}) collective-permute-start(bf16[16,40,128]{2,1,0:T(8,128)(2,1)S(1)} %slice.284), channel_id=1, source_target_pairs={{0,16},{1,17},{2,18},{3,19},{4,20},{5,21},{6,22},{7,23},{8,24},{9,... | collective-permute-start | bytes 491528 | tf_op jit(solution)/shard_map/ppermute | solution.py:390
  172.2 5.4 %collective-permute-start.29 = (bf16[16,40,128]{2,1,0:T(8,128)(2,1)S(1)}, bf16[16,40,128]{2,1,0:T(8,128)(2,1)S(1)}, u32[]{:S(2)}, u32[]{:S(2)}) collective-permute-start(bf16[16,40,128]{2,1,0:T(8,128)(2,1)S(1)} %slice.283), channel_id=1, source_target_pairs={{0,1},{1,0},{2,3},{3,2},{4,5},{5,4},{6,7},{7,6},{8,9},{9,8},{10,11... | collective-permute-start | bytes 491528 | tf_op jit(solution)/shard_map/ppermute | solution.py:390
  173.3 5.4 %collective-permute-start.32 = (bf16[16,40,128]{2,1,0:T(8,128)(2,1)S(1)}, bf16[16,40,128]{2,1,0:T(8,128)(2,1)S(1)}, u32[]{:S(2)}, u32[]{:S(2)}) collective-permute-start(bf16[16,40,128]{2,1,0:T(8,128)(2,1)S(1)} %slice.282), channel_id=1, source_target_pairs={{0,4},{1,5},{2,6},{3,7},{4,0},{5,1},{6,2},{7,3},{8,12},{9,13},{10,... | collective-permute-start | bytes 491528 | tf_op jit(solution)/shard_map/ppermute | solution.py:390
  178.8 6.2 %collective-permute-start.33 = (bf16[3,4,40,128]{3,2,1,0:T(8,128)(2,1)S(1)}, bf16[3,4,40,128]{3,2,1,0:T(8,128)(2,1)S(1)}, u32[]{:S(2)}, u32[]{:S(2)}) collective-permute-start(bf16[3,4,40,128]{3,2,1,0:T(8,128)(2,1)S(1)} %get-tuple-element.80), channel_id=1, source_target_pairs={{0,12},{1,13},{2,14},{3,15},{4,8},{5,9},{6,10},{7,11},{8,4},{9,5},... | collective-permute-start | bytes 368648 | tf_op jit(solution)/shard_map/ppermute | solution.py:390
  180.3 7.0 %collective-permute-start.35 = (bf16[3,4,40,128]{3,2,1,0:T(8,128)(2,1)S(1)}, bf16[3,4,40,128]{3,2,1,0:T(8,128)(2,1)S(1)}, u32[]{:S(2)}, u32[]{:S(2)}) collective-permute-start(bf16[3,4,40,128]{3,2,1,0:T(8,128)(2,1)S(1)} %get-tuple-element.81), channel_id=1, source_target_pairs={{0,15},{1,14},{2,13},{3,12},{4,11},{5,10},{6,9},{7,8},{8,7},{9,6},... | collective-permute-start | bytes 368648 | tf_op jit(solution)/shard_map/ppermute | solution.py:390
  182.5 5.3 %collective-permute-start.34 = (bf16[3,4,40,128]{3,2,1,0:T(8,128)(2,1)S(1)}, bf16[3,4,40,128]{3,2,1,0:T(8,128)(2,1)S(1)}, u32[]{:S(2)}, u32[]{:S(2)}) collective-permute-start(bf16[3,4,40,128]{3,2,1,0:T(8,128)(2,1)S(1)} %get-tuple-element.82), channel_id=1, source_target_pairs={{0,3},{1,2},{2,1},{3,0},{4,7},{5,6},{6,5},{7,4},{8,11},{9,10},{10,... | collective-permute-start | bytes 368648 | tf_op jit(solution)/shard_map/ppermute | solution.py:390
  187.9 8.2 %collective-permute-start.36 = (bf16[3,4,40,128]{3,2,1,0:T(8,128)(2,1)S(1)}, bf16[3,4,40,128]{3,2,1,0:T(8,128)(2,1)S(1)}, u32[]{:S(2)}, u32[]{:S(2)}) collective-permute-start(bf16[3,4,40,128]{3,2,1,0:T(8,128)(2,1)S(1)} %fusion.3), channel_id=1, source_target_pairs={{0,112},{1,113},{2,114},{3,115},{4,116},{5,117},{6,118},{7,119},{8... | collective-permute-start | bytes 368648 | tf_op jit(solution)/shard_map/ppermute | solution.py:390
  196.1 6.8 %collective-permute-start.37 = (bf16[3,4,40,128]{3,2,1,0:T(8,128)(2,1)S(1)}, bf16[3,4,40,128]{3,2,1,0:T(8,128)(2,1)S(1)}, u32[]{:S(2)}, u32[]{:S(2)}) collective-permute-start(bf16[3,4,40,128]{3,2,1,0:T(8,128)(2,1)S(1)} %bitcast.86), channel_id=1, source_target_pairs={{0,48},{1,49},{2,50},{3,51},{4,52},{5,53},{6,54},{7,55},{8,56},{9,... | collective-permute-start | bytes 368648 | tf_op jit(solution)/shard_map/ppermute | solution.py:390
  202.9 7.8 %collective-permute-start.40 = (bf16[3,4,40,128]{3,2,1,0:T(8,128)(2,1)S(1)}, bf16[3,4,40,128]{3,2,1,0:T(8,128)(2,1)S(1)}, u32[]{:S(2)}, u32[]{:S(2)}) collective-permute-start(bf16[3,4,40,128]{3,2,1,0:T(8,128)(2,1)S(1)} %bitcast.81), channel_id=1, source_target_pairs={{0,15},{1,14},{2,13},{3,12},{4,11},{5,10},{6,9},{7,8},{8,7},{9,6},... | collective-permute-start | bytes 368648 | tf_op jit(solution)/shard_map/ppermute | solution.py:390
  204.8 6.0 %collective-permute-start.39 = (bf16[3,4,40,128]{3,2,1,0:T(8,128)(2,1)S(1)}, bf16[3,4,40,128]{3,2,1,0:T(8,128)(2,1)S(1)}, u32[]{:S(2)}, u32[]{:S(2)}) collective-permute-start(bf16[3,4,40,128]{3,2,1,0:T(8,128)(2,1)S(1)} %bitcast.82), channel_id=1, source_target_pairs={{0,3},{1,2},{2,1},{3,0},{4,7},{5,6},{6,5},{7,4},{8,11},{9,10},{10,... | collective-permute-start | bytes 368648 | tf_op jit(solution)/shard_map/ppermute | solution.py:390
  204.8 7.9 %collective-permute-start.38 = (bf16[3,4,40,128]{3,2,1,0:T(8,128)(2,1)S(1)}, bf16[3,4,40,128]{3,2,1,0:T(8,128)(2,1)S(1)}, u32[]{:S(2)}, u32[]{:S(2)}) collective-permute-start(bf16[3,4,40,128]{3,2,1,0:T(8,128)(2,1)S(1)} %bitcast.83), channel_id=1, source_target_pairs={{0,12},{1,13},{2,14},{3,15},{4,8},{5,9},{6,10},{7,11},{8,4},{9,5},... | collective-permute-start | bytes 368648 | tf_op jit(solution)/shard_map/ppermute | solution.py:390
  212.8 6.4 %collective-permute-start.41 = (bf16[16,40,128]{2,1,0:T(8,128)(2,1)S(1)}, bf16[16,40,128]{2,1,0:T(8,128)(2,1)S(1)}, u32[]{:S(2)}, u32[]{:S(2)}) collective-permute-start(bf16[16,40,128]{2,1,0:T(8,128)(2,1)S(1)} %get-tuple-element.79), channel_id=1, source_target_pairs={{0,16},{1,17},{2,18},{3,19},{4,20},{5,21},{6,22},{7,23},{8,24},{9,... | collective-permute-start | bytes 491528 | tf_op jit(solution)/shard_map/ppermute | solution.py:390
  215.6 6.9 %collective-permute-start.47 = (bf16[16,40,128]{2,1,0:T(8,128)(2,1)S(1)}, bf16[16,40,128]{2,1,0:T(8,128)(2,1)S(1)}, u32[]{:S(2)}, u32[]{:S(2)}) collective-permute-start(bf16[16,40,128]{2,1,0:T(8,128)(2,1)S(1)} %get-tuple-element.77), channel_id=1, source_target_pairs={{0,1},{1,0},{2,3},{3,2},{4,5},{5,4},{6,7},{7,6},{8,9},{9,8},{10,11... | collective-permute-start | bytes 491528 | tf_op jit(solution)/shard_map/ppermute | solution.py:390
  219.2 5.3 %collective-permute-start.44 = (bf16[16,40,128]{2,1,0:T(8,128)(2,1)S(1)}, bf16[16,40,128]{2,1,0:T(8,128)(2,1)S(1)}, u32[]{:S(2)}, u32[]{:S(2)}) collective-permute-start(bf16[16,40,128]{2,1,0:T(8,128)(2,1)S(1)} %get-tuple-element.78), channel_id=1, source_target_pairs={{0,4},{1,5},{2,6},{3,7},{4,0},{5,1},{6,2},{7,3},{8,12},{9,13},{10,... | collective-permute-start | bytes 491528 | tf_op jit(solution)/shard_map/ppermute | solution.py:390
  219.2 8.8 %collective-permute-start.42 = (bf16[32,40,128]{2,1,0:T(8,128)(2,1)S(1)}, bf16[32,40,128]{2,1,0:T(8,128)(2,1)S(1)}, u32[]{:S(2)}, u32[]{:S(2)}) collective-permute-start(bf16[32,40,128]{2,1,0:T(8,128)(2,1)S(1)} %pad_maximum_fusion.5), channel_id=1, source_target_pairs={{0,4},{1,5},{2,6},{3,7},{4,0},{5,1},{6,2},{7,3},{8,12},{9,13},{10,... | collective-permute-start | bytes 983048 | tf_op jit(solution)/shard_map/ppermute | solution.py:390
  222.5 7.7 %collective-permute-start.48 = (bf16[32,40,128]{2,1,0:T(8,128)(2,1)S(1)}, bf16[32,40,128]{2,1,0:T(8,128)(2,1)S(1)}, u32[]{:S(2)}, u32[]{:S(2)}) collective-permute-start(bf16[32,40,128]{2,1,0:T(8,128)(2,1)S(1)} %pad_maximum_fusion.7), channel_id=1, source_target_pairs={{0,16},{1,17},{2,18},{3,19},{4,20},{5,21},{6,22},{7,23},{8,24},{9,... | collective-permute-start | bytes 983048 | tf_op jit(solution)/shard_map/ppermute | solution.py:390
  224.5 7.2 %collective-permute-start.45 = (bf16[32,40,128]{2,1,0:T(8,128)(2,1)S(1)}, bf16[32,40,128]{2,1,0:T(8,128)(2,1)S(1)}, u32[]{:S(2)}, u32[]{:S(2)}) collective-permute-start(bf16[32,40,128]{2,1,0:T(8,128)(2,1)S(1)} %pad_maximum_fusion.6), channel_id=1, source_target_pairs={{0,1},{1,0},{2,3},{3,2},{4,5},{5,4},{6,7},{7,6},{8,9},{9,8},{10,11... | collective-permute-start | bytes 983048 | tf_op jit(solution)/shard_map/ppermute | solution.py:390
  228.1 14.7 %collective-permute-start.43 = (bf16[64,40,128]{2,1,0:T(8,128)(2,1)S(1)}, bf16[64,40,128]{2,1,0:T(8,128)(2,1)S(1)}, u32[]{:S(2)}, u32[]{:S(2)}) collective-permute-start(bf16[64,40,128]{2,1,0:T(8,128)(2,1)S(1)} %pad_maximum_fusion.1.rest_0_), channel_id=1, source_target_pairs={{0,1},{1,0},{2,3},{3,2},{4,5},{5,4},{6,7},{7,6},{8,9},{9,8},{10,11... | collective-permute-start | bytes 1966088 | tf_op jit(solution)/shard_map/ppermute | solution.py:390
  230.2 10.7 %collective-permute-start.49 = (bf16[64,40,128]{2,1,0:T(8,128)(2,1)S(1)}, bf16[64,40,128]{2,1,0:T(8,128)(2,1)S(1)}, u32[]{:S(2)}, u32[]{:S(2)}) collective-permute-start(bf16[64,40,128]{2,1,0:T(8,128)(2,1)S(1)} %pad_maximum_fusion.3.rest_1_), channel_id=1, source_target_pairs={{0,4},{1,5},{2,6},{3,7},{4,0},{5,1},{6,2},{7,3},{8,12},{9,13},{10,... | collective-permute-start | bytes 1966088 | tf_op jit(solution)/shard_map/ppermute | solution.py:390
  231.7 11.0 %collective-permute-start.46 = (bf16[64,40,128]{2,1,0:T(8,128)(2,1)S(1)}, bf16[64,40,128]{2,1,0:T(8,128)(2,1)S(1)}, u32[]{:S(2)}, u32[]{:S(2)}) collective-permute-start(bf16[64,40,128]{2,1,0:T(8,128)(2,1)S(1)} %pad_maximum_fusion.2.rest_2_), channel_id=1, source_target_pairs={{0,16},{1,17},{2,18},{3,19},{4,20},{5,21},{6,22},{7,23},{8,24},{9,... | collective-permute-start | bytes 1966088 | tf_op jit(solution)/shard_map/ppermute | solution.py:390
  (9 other events, 65.0 us)
